TPU v7x, 256 devices: a whole 4x4x8 slice. The times are simulated.
256 devices in a mesh: req: 32 (over z, y), tp: 8 (over x, core).
Axes of the slice: x: 4, y: 4, z: 8, core: 2. Of those that a mesh axis runs over, the one named last changes fastest.
Arguments:
- ssm_input: bfloat16 [32, 512, 8192], P('req', 'tp'), may hold values from -6 to 6
- ssm_gate: bfloat16 [32, 512, 8192], P('req', 'tp'), may hold values from -6 to 6
- state_proj: bfloat16 [32, 512, 4096], P('req', 'tp'), may hold values from -1.796875 to 1.796875
- step_raw: bfloat16 [32, 512, 128], P('req', 'tp'), may hold values from -3 to 3
- queries: bfloat16 [32, 512, 4096], P('req', 'tp'), may hold values from -5 to 5
- fresh_kv: bfloat16 [32, 512, 2048], P('req', 'tp'), may hold values from -6 to 6
- block_pool: bfloat16 [128, 64, 8, 256], P('req', None, 'tp'), may hold values from -5 to 5
- state_pool: bfloat16 [32, 128, 64, 256], P('req', 'tp'), may hold values from -16 to 16
- decay_log: float32 [128], P('tp'), may hold values from -10 to -1
- step_bias: float32 [128], P('tp'), may hold values from -1 to 0
- skip_gain: float32 [128], P('tp'), may hold values from 1 to 3
- norm_gain: float32 [8192], P('tp'), may hold values from 0.5 to 1.5
- block_owner: int32 [32, 64], replicated, may hold values from 0 to 31, as said below
- block_slot: int32 [32, 64], replicated, may hold values from 0 to 3, as said below
- block_count: int32 [32], replicated, may hold values from 32 to 64, as said below
- state_entry: int32 [32], replicated, may hold values from 0 to 31
- suffix_len: int32 [32], replicated, may hold values from 128 to 512, as said below
Outputs:
- ssm_out: bfloat16 [32, 512, 8192], P('req', 'tp')
- attn_out: bfloat16 [32, 512, 4096], P('req', 'tp')
Inputs may be any that keep to these rules, and one draw needn't show every extreme that they name: `block_owner`: among the first block_count[r] entries of a request no owner appears more than 2 times; in every draw one request has 64 entries in use and takes exactly 2 from every owner. The owner at entry j is named again at entry j + 32. Requests 4k to 4k + 3 name the same owners at every entry. `block_slot`: requests 4k to 4k + 3 name the same blocks in their first 32 entries. `block_count`: some request has 64 in every draw. `suffix_len`: some request has 512 in every draw.
All inputs are finite; a program needn't handle non-finite values.
Results may differ from a plain program's by a relative error of at most 0.0048.
Values may be sent and summed in bfloat16 or wider, within the bound.
A program may use at most 128 MiB of HBM per device.

v0:
```python
import jax
import jax.numpy as jnp
from jax import lax
from jax.sharding import PartitionSpec as P

STATE = 256
SPAN = 256


def scan_heads(
    ssm_rows,
    gate_rows,
    proj_rows,
    step_rows,
    initial,
    decay_log,
    step_bias,
    skip_gain,
    norm_gain,
    live_len,
    group_count,
):
    length_all, width = ssm_rows.shape
    head_count = step_rows.shape[1]
    head_size = width // head_count
    per_group = head_count // group_count
    state_size = proj_rows.shape[1] // (2 * group_count)
    block_count = length_all // SPAN
    inputs = ssm_rows.reshape(block_count, SPAN, group_count, per_group, head_size)
    proj_four = proj_rows.reshape(block_count, SPAN, group_count, 2, state_size)
    in_proj = proj_four[:, :, :, 0]
    out_proj = proj_four[:, :, :, 1]
    step_size = jax.nn.softplus(step_rows.astype(jnp.float32) + step_bias[None, :])
    step_size = step_size.reshape(block_count, SPAN, group_count, per_group)
    rates = jnp.exp(decay_log).reshape(group_count, per_group)
    skip_heads = skip_gain.reshape(group_count, per_group)
    lower = jnp.arange(SPAN)[:, None] >= jnp.arange(SPAN)[None, :]

    def advance(state, block_in):
        block_x, block_b, block_c, block_dt = block_in
        cumul = jnp.cumsum(-rates[None] * block_dt, axis=0)
        inner = jnp.einsum("tgn,ugn->tug", block_c, block_b, preferred_element_type=jnp.float32)
        spread = cumul[:, None] - cumul[None, :]
        decay = jnp.exp(jnp.where(lower[:, :, None, None], spread, -jnp.inf))
        mixing = (decay * inner[:, :, :, None] * block_dt[None]).astype(jnp.bfloat16)
        output = jnp.einsum("tugh,ughp->tghp", mixing, block_x, preferred_element_type=jnp.float32)
        state_in = state.astype(jnp.bfloat16)
        carried = jnp.einsum(
            "tgn,ghpn->tghp", block_c, state_in, preferred_element_type=jnp.float32
        )
        output = output + jnp.exp(cumul)[..., None] * carried
        output = output + skip_heads[None, :, :, None] * block_x.astype(jnp.float32)
        tail_weight = jnp.exp(cumul[-1][None] - cumul) * block_dt
        tail_terms = (tail_weight[..., None] * block_x).astype(jnp.bfloat16)
        state = jnp.exp(cumul[-1])[:, :, None, None] * state + jnp.einsum(
            "ughp,ugn->ghpn", tail_terms, block_b, preferred_element_type=jnp.float32
        )
        return (state, output)

    start_state = initial.reshape(group_count, per_group, head_size, state_size)
    final_state, outputs = lax.scan(advance, start_state, (inputs, in_proj, out_proj, step_size))
    outputs = outputs.reshape(length_all, group_count, per_group * head_size)
    gated = outputs * jax.nn.silu(gate_rows.astype(jnp.float32)).reshape(
        length_all, group_count, per_group * head_size
    )
    mean_sq = jnp.mean(gated * gated, axis=-1, keepdims=True)
    normed = (
        gated * lax.rsqrt(mean_sq + 1e-05) * norm_gain.reshape(group_count, per_group * head_size)
    )
    normed = normed.reshape(length_all, width)
    alive = jnp.arange(length_all) < live_len
    return jnp.where(alive[:, None], normed, 0.0).astype(jnp.bfloat16)


def attend(query_rows, key_rows, value_rows, prefix_live, live_len):
    length_all, kv_count, repeat, head_size = query_rows.shape
    key_total = key_rows.shape[0]
    prefix_rows = key_total - length_all
    rows_block = min(256, length_all)
    inv_root = 1.0 / head_size**0.5
    key_index = jnp.arange(key_total)

    def one_block(offset):
        block_q = lax.dynamic_slice_in_dim(query_rows, offset, rows_block, 0)
        scores = (
            jnp.einsum("qcrd,kcd->crqk", block_q, key_rows, preferred_element_type=jnp.float32)
            * inv_root
        )
        query_index = offset + jnp.arange(rows_block)
        allowed = jnp.where(
            key_index[None, :] < prefix_rows,
            key_index[None, :] < prefix_live,
            key_index[None, :] - prefix_rows <= query_index[:, None],
        )
        scores = jnp.where(allowed[None, None], scores, -jnp.inf)
        row_max = jnp.max(scores, axis=-1, keepdims=True)
        expon = jnp.exp(scores - row_max)
        totals = jnp.sum(expon, axis=-1)
        weights = expon.astype(jnp.bfloat16)
        mixed = jnp.einsum(
            "crqk,kcd->qcrd", weights, value_rows, preferred_element_type=jnp.float32
        )
        mixed = mixed / jnp.transpose(totals, (2, 0, 1))[..., None]
        mixed = jnp.where((query_index < live_len)[:, None, None, None], mixed, 0.0)
        return mixed.astype(jnp.bfloat16)

    outputs = lax.map(one_block, jnp.arange(length_all // rows_block, dtype=jnp.int32) * rows_block)
    return outputs.reshape(length_all, kv_count * repeat * head_size)


def per_device(
    ssm_input,
    ssm_gate,
    state_proj,
    step_raw,
    queries,
    fresh_kv,
    block_pool,
    state_pool,
    decay_log,
    step_bias,
    skip_gain,
    norm_gain,
    block_owner,
    block_slot,
    block_count,
    state_entry,
    suffix_len,
):
    my_index = lax.axis_index("req")
    ssm_rows, gate_rows, proj_rows, step_rows, query_rows, fresh_rows = (
        lax.all_to_all(ssm_input, "tp", split_axis=2, concat_axis=1, tiled=True),
        lax.all_to_all(ssm_gate, "tp", split_axis=2, concat_axis=1, tiled=True),
        lax.all_to_all(state_proj, "tp", split_axis=2, concat_axis=1, tiled=True),
        lax.all_to_all(step_raw, "tp", split_axis=2, concat_axis=1, tiled=True),
        lax.all_to_all(queries, "tp", split_axis=2, concat_axis=1, tiled=True),
        lax.all_to_all(fresh_kv, "tp", split_axis=2, concat_axis=1, tiled=True),
    )
    wanted = state_entry[my_index]
    shard_rows = lax.all_gather(state_pool, "req", axis=0, tiled=True)
    marks = (jnp.arange(shard_rows.shape[0]) == wanted).astype(jnp.bfloat16)
    initial = jnp.einsum("e,emdn->mdn", marks, shard_rows, preferred_element_type=jnp.float32)
    live_len = suffix_len[my_index]
    local_groups = state_proj.shape[2] // (2 * STATE) // lax.axis_size("tp")
    mamba = scan_heads(
        ssm_rows[0],
        gate_rows[0],
        proj_rows[0],
        step_rows[0],
        initial,
        decay_log,
        step_bias,
        skip_gain,
        norm_gain,
        live_len,
        local_groups,
    )
    owners_row = block_owner[my_index]
    slots_row = block_slot[my_index]
    pool_local = block_pool.shape[0]
    table_len = block_owner.shape[1]
    targets = owners_row * pool_local + slots_row
    blank_blocks = jnp.zeros((table_len,) + block_pool.shape[1:], jnp.bfloat16)
    shard_rows = lax.all_gather(block_pool, "req", axis=0, tiled=True)
    inside = (targets >= 0) & (targets < shard_rows.shape[0])
    taken = shard_rows[jnp.clip(targets, 0, shard_rows.shape[0] - 1)]
    fetched = jnp.where(inside[:, None, None, None], taken, blank_blocks)
    kv_local = block_pool.shape[2]
    head_size = block_pool.shape[3] // 2
    length_all = ssm_rows.shape[1]
    cached = fetched.reshape(table_len * block_pool.shape[1], kv_local, 2 * head_size)
    newest = fresh_rows[0].reshape(length_all, kv_local, 2 * head_size)
    joined = jnp.concatenate([cached, newest], axis=0)
    grouped_q = query_rows[0].reshape(length_all, kv_local, -1, head_size)
    attention = attend(
        grouped_q,
        joined[..., :head_size],
        joined[..., head_size:],
        block_count[my_index] * block_pool.shape[1],
        live_len,
    )
    ssm_out, attn_out = (
        lax.all_to_all(mamba[None], "tp", split_axis=1, concat_axis=2, tiled=True),
        lax.all_to_all(attention[None], "tp", split_axis=1, concat_axis=2, tiled=True),
    )
    return (ssm_out, attn_out)


def solution(mesh):
    return jax.shard_map(
        per_device,
        mesh=mesh,
        in_specs=(
            P("req", "tp", None),
            P("req", "tp", None),
            P("req", "tp", None),
            P("req", "tp", None),
            P("req", "tp", None),
            P("req", "tp", None),
            P("req", None, "tp", None),
            P("req", "tp", None, None),
            P("tp"),
            P("tp"),
            P("tp"),
            P("tp"),
            P(),
            P(),
            P(),
            P(),
            P(),
        ),
        out_specs=(P("req", "tp", None), P("req", "tp", None)),
        check_vma=False,
    )
```

profile of v0, /device:TPU:1, one launch (start us, length us, event | category | flops | bytes accessed | tf_op | source)
XLA Modules:
  0.0 442.8 jit_solution(2404893305456525142)
XLA Ops:
  11.6 6.5 %all-to-all-start = ((bf16[8,2,512]{2,1,0:T(2,128)(2,1)}), bf16[8,2,512]{2,1,0:T(2,128)(2,1)S(1)}, u32[]{:S(2)}, u32[]{:S(2)}) async-start(bf16[8,2,512]{2,1,0:T(2,128)(2,1)} %reshape.753), calls=%async_computation | async-start | bytes 32768 | tf_op jit(solution)/shard_map/all_to_all | solution.py:135
  18.1 2.3 copy.208
  20.4 11.6 %reduce.20 = bf16[2048,64]{1,0:T(8,128)(2,1)S(1)} reduce(bf16[2048,1,64]{2,1,0:T(2,128)(2,1)S(1)} %bitcast.378, bf16[]{:T(256)} %broadcast.479), dimensions={1}, to_apply=%bitcast.275.reduce_sub_computation | reduce | bytes 524290
  33.1 5.2 %all-to-all-start.6 = ((bf16[8,2,8192]{2,1,0:T(2,128)(2,1)}), bf16[8,2,8192]{2,1,0:T(2,128)(2,1)S(1)}, u32[]{:S(2)}, u32[]{:S(2)}) async-start(bf16[8,2,8192]{2,1,0:T(2,128)(2,1)} %reshape.765), calls=%async_computation.6 | async-start | bytes 524288 | tf_op jit(solution)/shard_map/all_to_all | solution.py:137
  38.3 2.8 copy.187
  41.1 22.5 %reduce.16 = bf16[4096,64]{1,0:T(8,128)(2,1)S(1)} reduce(bf16[4096,1,64]{2,1,0:T(2,128)(2,1)S(1)} %bitcast.369, bf16[]{:T(256)} %broadcast.479), dimensions={1}, to_apply=%bitcast.267.reduce_sub_computation | reduce | bytes 1048578
  63.5 1.5 reshape.757
  65.0 5.4 %all-to-all-start.2 = ((bf16[8,2,16384]{2,1,0:T(2,128)(2,1)}), bf16[8,2,16384]{2,1,0:T(2,128)(2,1)}, u32[]{:S(2)}, u32[]{:S(2)}) async-start(bf16[8,2,16384]{2,1,0:T(2,128)(2,1)} %reshape.757), calls=%async_computation.2 | async-start | bytes 1048576 | tf_op jit(solution)/shard_map/all_to_all | solution.py:134
  70.5 4.9 %copy.205 = bf16[1,64,4096]{1,0,2:T(2,128)(2,1)S(1)} copy(bf16[1,64,4096]{2,1,0:T(8,128)(2,1)} %param.25) | data formatting | bytes 1048576 | tf_op args[4]
  75.4 22.5 %reduce.19 = bf16[4096,64]{1,0:T(8,128)(2,1)S(1)} reduce(bf16[4096,1,64]{2,1,0:T(2,128)(2,1)S(1)} %bitcast.370, bf16[]{:T(256)} %broadcast.479), dimensions={1}, to_apply=%bitcast.273.reduce_sub_computation | reduce | bytes 1048578
  97.9 1.5 reshape.763
  100.1 5.0 %all-to-all-start.5 = ((bf16[8,2,16384]{2,1,0:T(2,128)(2,1)}), bf16[8,2,16384]{2,1,0:T(2,128)(2,1)S(1)}, u32[]{:S(2)}, u32[]{:S(2)}) async-start(bf16[8,2,16384]{2,1,0:T(2,128)(2,1)} %reshape.763), calls=%async_computation.5 | async-start | bytes 1048576 | tf_op jit(solution)/shard_map/all_to_all | solution.py:136
  105.8 6.8 %copy.184 = bf16[1,64,8192]{1,0,2:T(2,128)(2,1)} copy(bf16[1,64,8192]{2,1,0:T(8,128)(2,1)S(1)} %copy-done.11) | data formatting | bytes 2097152 | tf_op args[0]
  112.6 45.3 %reduce.15 = bf16[8192,64]{1,0:T(8,128)(2,1)S(1)} reduce(bf16[8192,1,64]{2,1,0:T(2,128)(2,1)} %bitcast.364, bf16[]{:T(256)} %broadcast.479), dimensions={1}, to_apply=%bitcast.265.reduce_sub_computation | reduce | bytes 2097154
  157.9 2.7 reshape.755
  160.6 9.2 %copy.195 = bf16[1,64,8192]{1,0,2:T(2,128)(2,1)} copy(bf16[1,64,8192]{2,1,0:T(8,128)(2,1)} %param.22) | data formatting | bytes 2097152 | tf_op args[1]
  169.8 45.5 %reduce.17 = bf16[8192,64]{1,0:T(8,128)(2,1)S(1)} reduce(bf16[8192,1,64]{2,1,0:T(2,128)(2,1)} %bitcast.365, bf16[]{:T(256)} %broadcast.479), dimensions={1}, to_apply=%bitcast.269.reduce_sub_computation | reduce | bytes 2097154
  215.3 2.7 reshape.759
  222.7 4.8 %all-to-all-start.1 = ((bf16[8,2,32768]{2,1,0:T(2,128)(2,1)}), bf16[8,2,32768]{2,1,0:T(2,128)(2,1)S(1)}, u32[]{:S(2)}, u32[]{:S(2)}) async-start(bf16[8,2,32768]{2,1,0:T(2,128)(2,1)} %reshape.755), calls=%async_computation.1 | async-start | bytes 2097152 | tf_op jit(solution)/shard_map/all_to_all | solution.py:132
  229.7 4.1 reshape.758
  233.9 3.6 copy.188
  237.5 2.0 copy.232
  239.5 4.1 reshape.764
  243.7 3.6 copy.206
  247.3 1.2 copy.235
  249.6 4.8 %all-to-all-start.3 = ((bf16[8,2,32768]{2,1,0:T(2,128)(2,1)}), bf16[8,2,32768]{2,1,0:T(2,128)(2,1)}, u32[]{:S(2)}, u32[]{:S(2)}) async-start(bf16[8,2,32768]{2,1,0:T(2,128)(2,1)} %reshape.759), calls=%async_computation.3 | async-start | bytes 2097152 | tf_op jit(solution)/shard_map/all_to_all | solution.py:133
  256.7 4.4 reshape.756
  261.1 8.2 %copy.185 = bf16[1,64,8192]{2,1,0:T(8,128)(2,1)S(1)} copy(bf16[1,64,8192]{1,0,2:T(2,128)(2,1)} %bitcast.362) | data formatting | bytes 2097152 | tf_op jit(solution)/shard_map/all_to_all | solution.py:132
  269.9 1.5 copy.186
  271.5 2.9 reshape_squeeze.12
  274.4 2.5 copy.191
  276.9 6.5 %reshape.760 = bf16[8192,1,64]{2,1,0:T(2,128)(2,1)} reshape(bf16[8,2,32768]{2,1,0:T(2,128)(2,1)} %all-to-all-done.3) | data formatting | bytes 2097152
  283.5 8.2 %copy.196 = bf16[1,64,8192]{2,1,0:T(8,128)(2,1)S(1)} copy(bf16[1,64,8192]{1,0,2:T(2,128)(2,1)} %bitcast.363) | data formatting | bytes 2097152 | tf_op jit(solution)/shard_map/all_to_all | solution.py:133
  292.5 1.2 copy.197
  293.8 2.5 reshape.716
  296.3 4.5 %copy.202 = f32[2,256,1,16,64]{1,4,3,2,0:T(8,128)} copy(f32[2,256,1,16,64]{4,3,1,0,2:T(8,128)} %reshape.716) | data formatting | bytes 4194304 | tf_op jit(solution)/shard_map/convert_element_type | solution.py:63
  300.9 1.8 copy.199
  302.7 2.9 gather_fusion
  305.6 2.1 bitcast_select_fusion.1
  307.7 1.2 pad_maximum_fusion
  308.9 43.2 %while.30 = (s32[]{:T(128)}, bf16[2,256,1,4,128]{4,3,1,0,2:T(4,128)(2,1)S(1)}, s32[2]{0:T(128)S(1)}, s32[]{:T(128)}, s32[]{:T(128)}, /*index=5*/bf16[512,1,4,128...) while((s32[]{:T(128)}, ...), condition=%wide.region_8.9_spmd.clone.clone, body=%wide.region_5.8_spmd.clone.clone.sunk | while | flops 2470588672 | bytes 65352372 | solution.py:107
  313.5 5.0 %fusion.115 = (f32[4,256]{1,0:T(4,128)S(1)}, f32[256,4,4608]{2,0,1:T(8,128)S(1)}) fusion(pred[256,4608]{1,0:T(8,128)(4,1)S(1)} %compare_select_fusion.4, bf16[4608,1,128]{2,0,1:T(8,128)(2,1)} %get-tuple-element.639, bf16[256,1,4,128]{3,2,0,1:T(4,128)(2,1)S(1)} %constant_dynamic-slice_fusion.4), kind=kOutput, calls=%fused_computation.7.clone.1 | convolution fusion | flops 1222114304 | bytes 21499904 | tf_op jit(solution)/shard_map/while/body/eval_jaxpr/qcrd,kcd->crqk/dot_general | solution.py:86
  318.5 5.0 %fusion.116 = f32[4,256]{1,0:T(4,128)S(1)} fusion(f32[256,4,4608]{2,0,1:T(8,128)S(1)} %get-tuple-element.576, f32[4,256]{1,0:T(4,128)S(1)} %get-tuple-element.577, pred[256,4608]{1,0:T(8,128)(4,1)S(1)} %compare_select_fusion.4), kind=kLoop, calls=%fused_computation.5.clone.1 | loop fusion | flops 18873344 | bytes 20062208 | tf_op jit(solution)/shard_map/while/body/eval_jaxpr/reduce_sum | solution.py:98
  323.4 1.3 broadcast_compare_fusion.2
  324.7 5.7 %fusion.117 = bf16[1,256,1,4,128]{4,1,3,2,0:T(8,128)(2,1)S(1)} fusion(bf16[4608,1,128]{2,0,1:T(8,128)(2,1)S(1)} %get-tuple-element.640, f32[256,4,4608]{2,0,1:T(8,128)S(1)} %get-tuple-element.576, f32[4,256]{1,0:T(4,128)S(1)} %get-tuple-element.577, pred[256,4608]{1,0:T(8,128)(4,1)S(1)} %compare_select_fusion.4, f32[256,4]{0,1:T(4,128)S(1)} %bitcast.400, ...), kind=kOutput, calls=%fused_computation.19.clone.1 | convolution fusion | flops 1227227136 | bytes 21504256 | tf_op jit(solution)/shard_map/while/body/eval_jaxpr/crqk,kcd->qcrd/dot_general | solution.py:100
  334.9 5.0 %fusion.115 = (f32[4,256]{1,0:T(4,128)S(1)}, f32[256,4,4608]{2,0,1:T(8,128)S(1)}) fusion(pred[256,4608]{1,0:T(8,128)(4,1)S(1)} %compare_select_fusion.4, bf16[4608,1,128]{2,0,1:T(8,128)(2,1)} %get-tuple-element.639, bf16[256,1,4,128]{3,2,0,1:T(4,128)(2,1)S(1)} %constant_dynamic-slice_fusion.4), kind=kOutput, calls=%fused_computation.7.clone.1 | convolution fusion | flops 1222114304 | bytes 21499904 | tf_op jit(solution)/shard_map/while/body/eval_jaxpr/qcrd,kcd->crqk/dot_general | solution.py:86
  339.9 5.0 %fusion.116 = f32[4,256]{1,0:T(4,128)S(1)} fusion(f32[256,4,4608]{2,0,1:T(8,128)S(1)} %get-tuple-element.576, f32[4,256]{1,0:T(4,128)S(1)} %get-tuple-element.577, pred[256,4608]{1,0:T(8,128)(4,1)S(1)} %compare_select_fusion.4), kind=kLoop, calls=%fused_computation.5.clone.1 | loop fusion | flops 18873344 | bytes 20062208 | tf_op jit(solution)/shard_map/while/body/eval_jaxpr/reduce_sum | solution.py:98
  344.9 1.3 broadcast_compare_fusion.2
  346.2 5.7 %fusion.117 = bf16[1,256,1,4,128]{4,1,3,2,0:T(8,128)(2,1)S(1)} fusion(bf16[4608,1,128]{2,0,1:T(8,128)(2,1)S(1)} %get-tuple-element.640, f32[256,4,4608]{2,0,1:T(8,128)S(1)} %get-tuple-element.576, f32[4,256]{1,0:T(4,128)S(1)} %get-tuple-element.577, pred[256,4608]{1,0:T(8,128)(4,1)S(1)} %compare_select_fusion.4, f32[256,4]{0,1:T(4,128)S(1)} %bitcast.400, ...), kind=kOutput, calls=%fused_computation.19.clone.1 | convolution fusion | flops 1227227136 | bytes 21504256 | tf_op jit(solution)/shard_map/while/body/eval_jaxpr/crqk,kcd->qcrd/dot_general | solution.py:100
  352.4 3.9 reduce.21
  357.4 5.0 %all-to-all-start.7 = ((bf16[8,2,16384]{2,1,0:T(2,128)(2,1)}), bf16[8,2,16384]{2,1,0:T(2,128)(2,1)}, u32[]{:S(2)}, u32[]{:S(2)}) async-start(bf16[8,2,16384]{2,1,0:T(2,128)(2,1)} %reshape.767), calls=%async_computation.7 | async-start | bytes 1048576 | tf_op jit(solution)/shard_map/all_to_all | solution.py:184
  362.5 15.8 %fusion.76 = f32[1,16,64,256]{3,0,2,1:T(1,128)S(1)} fusion(bf16[32,16,64,256]{3,2,1,0:T(8,128)(2,1)} %all-gather.3.cloned.1.call-done, s32[]{:T(128)} %bitcast.1), kind=kOutput, calls=%fused_computation.84 | convolution fusion | flops 16777248 | bytes 17825796 | tf_op jit(solution)/shard_map/e,emdn->mdn/dot_general | solution.py:142
  379.7 11.0 %while.29 = (s32[]{:T(128)}, f32[1,16,64,256]{3,2,1,0:T(8,128)S(1)}, f32[2,256,1,16,64]{1,4,3,2,0:T(8,128)}, f32[1,1,16]{2,1,0:T(1,128)S(1)}, f32[2,256,1,16]{1,...) while((s32[]{:T(128)}, ...), condition=%wide.region_3.4_spmd.clone, body=%wide.region_0.3_spmd.clone.sunk | while | flops 444936256 | bytes 26842868 | solution.py:61
  381.5 1.2 fusion.111
  386.9 1.2 fusion.111
  390.7 4.7 %copy.194 = f32[2,256,1,16,64]{1,0,4,3,2:T(2,128)} copy(f32[2,256,1,16,64]{1,4,3,2,0:T(8,128)} %get-tuple-element.237) | data formatting | bytes 4194304 | tf_op jit(solution)/shard_map/while | solution.py:61
  396.2 4.1 reshape.708
  400.3 2.4 select_convert_fusion
  402.7 2.2 copy.203
  404.9 6.8 %reduce.18 = bf16[512,1024]{1,0:T(8,128)(2,1)S(1)} reduce(bf16[512,1,1024]{2,1,0:T(2,128)(2,1)S(1)} %bitcast.371, bf16[]{:T(256)} %broadcast.479), dimensions={1}, to_apply=%bitcast.271.reduce_sub_computation | reduce | bytes 2097154
  411.7 1.6 reshape.761
  413.3 4.8 %all-to-all-start.4 = ((bf16[8,2,32768]{2,1,0:T(2,128)(2,1)}), bf16[8,2,32768]{2,1,0:T(2,128)(2,1)S(1)}, u32[]{:S(2)}, u32[]{:S(2)}) async-start(bf16[8,2,32768]{2,1,0:T(2,128)(2,1)} %reshape.761), calls=%async_computation.4 | async-start | bytes 2097152 | tf_op jit(solution)/shard_map/all_to_all | solution.py:183
  418.1 2.2 reshape.768
  421.3 11.9 %all-to-all-done.4 = bf16[8,2,32768]{2,1,0:T(2,128)(2,1)S(1)} async-done(((bf16[8,2,32768]{2,1,0:T(2,128)(2,1)}), bf16[8,2,32768]{2,1,0:T(2,128)(2,1)S(1)}, u32[]{:S(2)}, u32[]{:S(2)}) %all-to-all-start.4) | async-done | bytes 1048608 | tf_op jit(solution)/shard_map/all_to_all | solution.py:183
  (173 shorter events, 38.0 us)
Async XLA Ops:
  7.2 295.5 %all-gather.5.cloned.1.call-start = ((), (), s32[]{:S(2)}) async-start(), calls=%async_computation.9 | async-start | bytes 4325376 | tf_op jit(solution)/shard_map/all_gather | solution.py:164
  7.9 354.6 %all-gather.3.cloned.1.call-start = ((), (), s32[]{:S(2)}) async-start(), calls=%async_computation.8 | async-start | bytes 17301504 | tf_op jit(solution)/shard_map/all_gather | solution.py:140
  11.6 21.4 %all-to-all-start = ((bf16[8,2,512]{2,1,0:T(2,128)(2,1)}), bf16[8,2,512]{2,1,0:T(2,128)(2,1)S(1)}, u32[]{:S(2)}, u32[]{:S(2)}) async-start(bf16[8,2,512]{2,1,0:T(2,128)(2,1)} %reshape.753), calls=%async_computation | async-start | bytes 32768 | tf_op jit(solution)/shard_map/all_to_all | solution.py:135
  18.1 20.1 %copy-start.12 = (bf16[1,64,4096]{2,1,0:T(8,128)(2,1)S(1)}, bf16[1,64,4096]{2,1,0:T(8,128)(2,1)}, u32[]{:S(2)}) copy-start(bf16[1,64,4096]{2,1,0:T(8,128)(2,1)} %param.23) | copy-start | bytes 1572868
  33.1 32.0 %all-to-all-start.6 = ((bf16[8,2,8192]{2,1,0:T(2,128)(2,1)}), bf16[8,2,8192]{2,1,0:T(2,128)(2,1)S(1)}, u32[]{:S(2)}, u32[]{:S(2)}) async-start(bf16[8,2,8192]{2,1,0:T(2,128)(2,1)} %reshape.765), calls=%async_computation.6 | async-start | bytes 524288 | tf_op jit(solution)/shard_map/all_to_all | solution.py:137
  65.0 35.1 %all-to-all-start.2 = ((bf16[8,2,16384]{2,1,0:T(2,128)(2,1)}), bf16[8,2,16384]{2,1,0:T(2,128)(2,1)}, u32[]{:S(2)}, u32[]{:S(2)}) async-start(bf16[8,2,16384]{2,1,0:T(2,128)(2,1)} %reshape.757), calls=%async_computation.2 | async-start | bytes 1048576 | tf_op jit(solution)/shard_map/all_to_all | solution.py:134
  97.8 7.3 %copy-start.20 = (s32[32]{0:T(128)S(1)}, s32[32]{0:T(128)}, u32[]{:S(2)}) copy-start(s32[32]{0:T(128)} %param.36) | copy-start | bytes 388
  97.9 8.0 %copy-start.11 = (bf16[1,64,8192]{2,1,0:T(8,128)(2,1)S(1)}, bf16[1,64,8192]{2,1,0:T(8,128)(2,1)}, u32[]{:S(2)}) copy-start(bf16[1,64,8192]{2,1,0:T(8,128)(2,1)} %param.21) | copy-start | bytes 3145732
  100.1 121.7 %all-to-all-start.5 = ((bf16[8,2,16384]{2,1,0:T(2,128)(2,1)}), bf16[8,2,16384]{2,1,0:T(2,128)(2,1)S(1)}, u32[]{:S(2)}, u32[]{:S(2)}) async-start(bf16[8,2,16384]{2,1,0:T(2,128)(2,1)} %reshape.763), calls=%async_computation.5 | async-start | bytes 1048576 | tf_op jit(solution)/shard_map/all_to_all | solution.py:136
  215.3 2.7 copy-start.21
  215.3 3.5 copy-start.22
  215.3 5.8 %copy-start.23 = (f32[16]{0:T(128)S(1)}, f32[16]{0:T(128)}, u32[]{:S(2)}) copy-start(f32[16]{0:T(128)} %param.29) | copy-start | bytes 196
  218.0 9.6 %copy-start.18 = (f32[16]{0:T(128)S(1)}, f32[16]{0:T(128)}, u32[]{:S(2)}) copy-start(f32[16]{0:T(128)} %param.30) | copy-start | bytes 196
  221.9 0.8 copy-start.10
  222.7 26.9 %all-to-all-start.1 = ((bf16[8,2,32768]{2,1,0:T(2,128)(2,1)}), bf16[8,2,32768]{2,1,0:T(2,128)(2,1)S(1)}, u32[]{:S(2)}, u32[]{:S(2)}) async-start(bf16[8,2,32768]{2,1,0:T(2,128)(2,1)} %reshape.755), calls=%async_computation.1 | async-start | bytes 2097152 | tf_op jit(solution)/shard_map/all_to_all | solution.py:132
  249.6 5.0 %copy-start.8 = (bf16[8,2,32768]{2,1,0:T(2,128)(2,1)}, bf16[8,2,32768]{2,1,0:T(2,128)(2,1)S(1)}, u32[]{:S(2)}) copy-start(bf16[8,2,32768]{2,1,0:T(2,128)(2,1)S(1)} %all-to-all-done.1) | copy-start | bytes 3145732
  249.6 27.4 %all-to-all-start.3 = ((bf16[8,2,32768]{2,1,0:T(2,128)(2,1)}), bf16[8,2,32768]{2,1,0:T(2,128)(2,1)}, u32[]{:S(2)}, u32[]{:S(2)}) async-start(bf16[8,2,32768]{2,1,0:T(2,128)(2,1)} %reshape.759), calls=%async_computation.3 | async-start | bytes 2097152 | tf_op jit(solution)/shard_map/all_to_all | solution.py:133
  255.0 1.7 copy-start.9
  307.7 1.2 copy-start.13
  357.4 55.9 %all-to-all-start.7 = ((bf16[8,2,16384]{2,1,0:T(2,128)(2,1)}), bf16[8,2,16384]{2,1,0:T(2,128)(2,1)}, u32[]{:S(2)}, u32[]{:S(2)}) async-start(bf16[8,2,16384]{2,1,0:T(2,128)(2,1)} %reshape.767), calls=%async_computation.7 | async-start | bytes 1048576 | tf_op jit(solution)/shard_map/all_to_all | solution.py:184
  378.3 1.2 copy-start
  378.3 1.3 copy-start.1
  378.3 1.3 copy-start.2
  378.3 1.3 copy-start.14
  378.3 1.3 copy-start.15
  378.3 1.3 copy-start.16
  381.4 1.6 copy-start.4
  383.4 1.4 copy-start.5
  386.9 1.6 copy-start.4
  388.8 1.4 copy-start.5
  390.7 4.7 %copy-start.3 = (f32[2,256,1,16,64]{1,4,3,2,0:T(8,128)S(1)}, f32[2,256,1,16,64]{1,4,3,2,0:T(8,128)}, u32[]{:S(2)}) copy-start(f32[2,256,1,16,64]{1,4,3,2,0:T(8,128)} %copy.202) | copy-start | bytes 6291460
  390.7 4.7 %copy-start.6 = (f32[2,256,1,16,64]{1,4,3,2,0:T(8,128)S(1)}, f32[2,256,1,16,64]{1,4,3,2,0:T(8,128)}, u32[]{:S(2)}) copy-start(f32[2,256,1,16,64]{1,4,3,2,0:T(8,128)} %get-tuple-element.237) | copy-start | bytes 6291460
  396.2 4.1 copy-start.7
  396.2 4.1 copy-start.17
  396.2 4.1 copy-start.19
  413.3 19.9 %all-to-all-start.4 = ((bf16[8,2,32768]{2,1,0:T(2,128)(2,1)}), bf16[8,2,32768]{2,1,0:T(2,128)(2,1)S(1)}, u32[]{:S(2)}, u32[]{:S(2)}) async-start(bf16[8,2,32768]{2,1,0:T(2,128)(2,1)} %reshape.761), calls=%async_computation.4 | async-start | bytes 2097152 | tf_op jit(solution)/shard_map/all_to_all | solution.py:183
Sparse Core Ops, SparseCore 0:
  10.6 82.9 all-gather.4
  96.2 140.1 all-gather.2
where the time goes:
time: 451 us; the launch traced here: 443 us
  other arithmetic  186 us (41%)
  local copies, waits for them, and re-layouts  140 us (31%)
  matrix products  41.9 us (9%)
  starting transfers between devices  41.6 us (9%)
  between operations  15.6 us (3%)
  waiting for transfers between devices  13.3 us (3%)
  loops' own time  4.89 us (1%)
    unnamed x9, other arithmetic  159 us
    unnamed x77, local copies, waits for them, and re-layouts  74 us
    dot_general x1, matrix products, per_device(): jnp.einsum('e,emdn->mdn', marks, shard_rows, preferred_element_type=jnp.f...  15.8 us
    all_to_all x1, waiting for transfers between devices, per_device(): lax.all_to_all(mamba[None], 'tp', split_axis=1, concat_axis=2, tiled=True)  11.9 us
    dot_general x2, matrix products, one_block(): jnp.einsum('crqk,kcd->qcrd', weights, value_rows, preferred_element_type=...  11.4 us
    convert_element_type x5, local copies, waits for them, and re-layouts, scan_heads(): gate_rows.astype(jnp.float32)  10.4 us
    dot_general x2, matrix products, one_block(): jnp.einsum('qcrd,kcd->crqk', block_q, key_rows, preferred_element_type=jn...  10 us
    reduce_sum x2, other arithmetic, one_block(): totals = jnp.sum(expon, axis=-1)  9.9 us
  transfers between devices with their start and end apart: 10, of which 1 were waited for; matrix products, arithmetic and copies ran while one was open for 81% of the time, Pallas kernels for 0%

commit v1 on v0

v1 whole, which is shorter than its diff:
```python
import jax
import jax.numpy as jnp
from jax import lax
from jax.experimental import pallas as pl
from jax.experimental.pallas import tpu as pltpu
from jax.sharding import PartitionSpec as P

MESH = pl.DeviceIdType.MESH
F32 = jnp.float32
BF16 = jnp.bfloat16

NZ, NY, NT = 8, 4, 8
ROWS = 64
SPAN = 256
CHUNKS = 4
DIST = (0, 1, 2, 3, 4, -1, -2, -3)
LOW = -1e30
SCALE = 1.4426950408889634 / 128**0.5


def dot(a, b, dims=(((1,), (0,)), ((), ())), precision=None):
    return lax.dot_general(a, b, dims, precision=precision, preferred_element_type=F32)


BT = (((1,), (1,)), ((), ()))
AT = (((0,), (0,)), ((), ()))


def kernel(
    tab,
    bias,
    par,
    gain,
    step,
    proj,
    xin,
    query,
    fresh,
    gate,
    pool,
    state,
    ssm_out,
    attn_out,
    stepb,
    gainb,
    projb,
    xb,
    qb,
    fb,
    gateb,
    kz,
    ksend,
    kvb,
    yb,
    tk,
    ts,
    cum_c,
    dt_c,
    w_c,
    cum_r,
    dt_r,
    inner,
    yint,
    ecx,
    tailb,
    osend,
    ob,
    m_s,
    l_s,
    acc_s,
    ao,
    lsem,
    xs,
    xr,
    kzs,
    kzr,
    kys,
    kyr,
    sys_,
    syr,
    tss,
    tsr,
    oss,
    osr,
    aos,
    aor,
):
    r = lax.axis_index("req")
    p = lax.axis_index("tp")
    z = r // NY
    y = lax.rem(r, NY)

    def tp_of(d):
        return lax.rem(p + d, NT)

    def z_of(k):
        return lax.rem(z + k + 2 * NZ, NZ)

    def y_of(k):
        return lax.rem(y + k + NY, NY)

    def remote(src, dst, ssem, rsem, device):
        return pltpu.make_async_remote_copy(
            src_ref=src, dst_ref=dst, send_sem=ssem, recv_sem=rsem, device_id=device, device_id_type=MESH
        )

    barrier = pltpu.get_barrier_semaphore()
    peers = [(r, tp_of(d)) for d in range(1, NT)]
    peers += [(z_of(1) * NY + y, p), (z_of(-1) * NY + y, p)]
    peers += [(z * NY + y_of(j), p) for j in range(1, NY)]
    for peer in peers:
        pl.semaphore_signal(barrier, inc=1, device_id=peer, device_id_type=MESH)
    pl.semaphore_wait(barrier, len(peers))

    pending = []
    local = []

    def start(copy):
        copy.start()
        pending.append(copy)
        return copy

    def start_local(src, dst):
        copy = pltpu.make_async_copy(src, dst, lsem.at[len(local)])
        copy.start()
        local.append(copy)
        return copy

    my_rows = pl.ds(pl.multiple_of(p * ROWS, ROWS), ROWS)

    def spread(i, src, dst, width):
        out = [start_local(src.at[:, pl.ds(pl.multiple_of(p * width, 128), width)], dst.at[my_rows, :])]
        for d in range(1, NT):
            to = tp_of(d)
            out.append(
                start(
                    remote(
                        src.at[:, pl.ds(pl.multiple_of(to * width, 128), width)],
                        dst.at[my_rows, :],
                        xs.at[i, d - 1],
                        xr.at[i, d - 1],
                        (r, to),
                    )
                )
            )
        return out

    def everyone(i, src, dst):
        out = [start_local(src, dst)]
        for d in range(1, NT):
            out.append(start(remote(src, dst, xs.at[i, d - 1], xr.at[i, d - 1], (r, tp_of(d)))))
        return out

    def arrive(copies):
        copies[0].wait()
        for copy in copies[1:]:
            copy.wait_recv()

    def gather_state(c):
        out = [start_local(state.at[c], yb[c].at[y])]
        for j in range(1, NY):
            out.append(
                start(
                    remote(
                        state.at[c],
                        yb[c].at[y],
                        sys_.at[c, j - 1],
                        syr.at[c, j - 1],
                        (z * NY + y_of(j), p),
                    )
                )
            )
        return out

    def kv_hop(s, way):
        slot = s if way > 0 else 4 + s
        before = pool if s == 1 else kz[slot - 1]
        return start(
            remote(before, kz[slot], kzs.at[slot], kzr.at[slot], (z_of(way) * NY + y, p))
        )

    kv_copies = {}

    def kv_across(k):
        for j in range(NY):
            to = y_of(j)
            first = kz[k][tab[0, to * 32 + k * 4 + y]]
            second = kz[k][tab[1, to * 32 + k * 4 + y]]
            if j == 0:
                kvb[y, k, 0] = first
                kvb[y, k, 1] = second
            else:
                ksend[k, j - 1, 0] = first
                ksend[k, j - 1, 1] = second
                kv_copies[k, j] = start(
                    remote(
                        ksend.at[k, j - 1],
                        kvb.at[y, k],
                        kys.at[k, j - 1],
                        kyr.at[k, j - 1],
                        (z * NY + to, p),
                    )
                )

    kv_hops = {}

    def kv_step(s):
        kv_hops[s, 1].wait_recv()
        if s < 4:
            kv_hops[s + 1, 1] = kv_hop(s + 1, 1)
        if s <= 3:
            kv_hops[s, -1].wait_recv()
            if s < 3:
                kv_hops[s + 1, -1] = kv_hop(s + 1, -1)
        kv_across(s)
        if s <= 3:
            kv_across(4 + s)

    gathers = {}
    tokens = {}

    def length(c, way):
        return 4 if (way > 0) == (c % 2 == 0) else 3

    def tok_hop(c, s, way):
        total = length(c, way)
        dest = z_of(way * (total - s + 1))
        base = 0 if way > 0 else 4
        mine = yb[c][tab[2, 8 + dest]]
        if s > 1:
            mine = jnp.where(tab[2, dest] == z, mine, tk[c][base + s - 2])
        ts[c][base + s - 1] = mine
        tokens[c, s, way] = start(
            remote(
                ts[c].at[base + s - 1],
                tk[c].at[base + s - 1],
                tss.at[c, base + s - 1],
                tsr.at[c, base + s - 1],
                (z_of(way) * NY + y, p),
            )
        )

    def tok_step(c, s):
        if s == 0:
            arrive(gathers[c])
            tok_hop(c, 1, 1)
            tok_hop(c, 1, -1)
            return
        for way in (1, -1):
            if s <= length(c, way):
                tokens[c, s, way].wait_recv()
                if s < length(c, way):
                    tok_hop(c, s + 1, way)

    gathers[0] = gather_state(0)
    kv_hops[1, 1] = kv_hop(1, 1)
    kv_hops[1, -1] = kv_hop(1, -1)
    in_step = everyone(0, step, stepb.at[my_rows, :])
    in_proj = spread(1, proj, projb, 512)
    in_x = spread(2, xin, xb, 1024)
    own_pool = start_local(pool, kz[0])
    in_gate = start_local(gate, gateb)
    own_pool.wait()
    kv_across(0)
    gathers[1] = gather_state(1)
    in_q = spread(3, query, qb, 512)
    in_f = spread(4, fresh, fb, 256)
    in_gain = everyone(5, gain, gainb.at[p])
    live = tab[2, 16]

    kv_step(1)
    kv_step(2)
    tok_step(0, 0)
    gathers[2] = gather_state(2)
    kv_step(3)
    tok_step(0, 1)

    arrive(in_step)
    take = (
        lax.broadcasted_iota(jnp.int32, (128, 128), 0)
        == lax.broadcasted_iota(jnp.int32, (128, 128), 1) + p * 16
    ).astype(BF16)
    raw = dot(stepb[...], take) + par[1:2, 0:128]
    dt = jnp.maximum(raw, 0.0) + jnp.log1p(jnp.exp(-jnp.abs(raw)))
    drop = dt * -jnp.exp(par[2:3, 0:128])
    lower = lax.broadcasted_iota(jnp.int32, (SPAN, SPAN), 0) >= lax.broadcasted_iota(
        jnp.int32, (SPAN, SPAN), 1
    )
    ones = lower.astype(F32)
    dt_c[...] = dt
    for b in range(2):
        rows = slice(b * SPAN, (b + 1) * SPAN)
        cum = dot(ones, drop[rows], precision=lax.Precision.HIGHEST)
        cum_c[rows, :] = cum
        cum_r[b] = cum.T
        dt_r[b] = dt[rows].T
        if b == 0:
            w_c[...] = jnp.exp(cum[SPAN - 1 : SPAN] - cum) * dt[rows]
    arrive(in_proj)
    for b in range(2):
        rows = slice(b * SPAN, (b + 1) * SPAN)
        inner[b] = dot(projb[rows, 256:512], projb[rows, 0:256], BT)
    arrive(in_x)

    half = lax.broadcasted_iota(jnp.int32, (SPAN, 128), 1) < 64

    def pair(hp, carry):
        cols = pl.ds(pl.multiple_of(hp * 128, 128), 128)
        for b in range(2):
            rows = slice(b * SPAN, (b + 1) * SPAN)
            xp = xb[rows, cols]
            cum_b = cum_c[rows, :]
            res, cumcols, weights = [], [], []
            for e in range(2):
                h = hp * 2 + e
                column = pltpu.roll(cum_b, 128 - h, 1)[:, 0:1]
                spread_cum = column - cum_r[b, pl.ds(h, 1), :]
                mix = jnp.exp(jnp.where(lower, spread_cum, LOW)) * inner[b] * dt_r[b, pl.ds(h, 1), :]
                res.append(dot(mix.astype(BF16), xp))
                cumcols.append(column)
                if b == 0:
                    weights.append(pltpu.roll(w_c[...], 128 - h, 1)[:, 0:1])
            xf = xp.astype(F32)
            ecx[rows, cols] = jnp.exp(jnp.where(half, cumcols[0], cumcols[1]))
            yint[rows, cols] = jnp.where(half, res[0], res[1]) + par[0:1, cols] * xf
            if b == 0:
                tailb[:, cols] = (jnp.where(half, weights[0], weights[1]) * xf).astype(BF16)
        return carry

    kv_step(4)
    tok_step(0, 2)
    tok_step(1, 0)
    gathers[3] = gather_state(3)
    lax.fori_loop(0, 4, pair, 0)
    tok_step(0, 3)
    tok_step(1, 1)
    lax.fori_loop(4, 8, pair, 0)

    def wait_out(copies):
        for copy in copies:
            copy.wait_recv()

    ssm_sends = {}

    def carry_in(c):
        ze = tab[2, z]
        behind = lax.rem(z - ze + NZ, NZ)
        entering = jnp.where(
            behind <= length(c, 1), tk[c][length(c, 1) - 1], tk[c][4 + length(c, -1) - 1]
        )
        s0 = jnp.where(ze == z, yb[c][tab[2, 8 + z]], entering)
        cols = slice(c * 256, (c + 1) * 256)
        eye = (
            lax.broadcasted_iota(jnp.int32, (256, 256), 0) == lax.broadcasted_iota(jnp.int32, (256, 256), 1)
        ).astype(BF16)
        s0t = dot(eye, s0, BT)
        s1t = ecx[SPAN - 1 : SPAN, cols] * s0t + dot(projb[0:SPAN, 0:256], tailb[:, cols], AT)
        for b, st in ((0, s0t), (1, s1t)):
            rows = slice(b * SPAN, (b + 1) * SPAN)
            carried = dot(projb[rows, 256:512], st.astype(BF16))
            osend[c, rows, :] = (yint[rows, cols] + ecx[rows, cols] * carried).astype(BF16)
        out = []
        for d in range(1, NT):
            to = tp_of(d)
            out.append(
                start(
                    remote(
                        osend.at[c, pl.ds(pl.multiple_of(to * ROWS, ROWS), ROWS), :],
                        ob.at[c, my_rows, :],
                        oss.at[c, d - 1],
                        osr.at[c, d - 1],
                        (r, to),
                    )
                )
            )
        ob[c, my_rows, :] = osend[c, my_rows, :]
        ssm_sends[c] = out

    tok_step(0, 4)
    tok_step(1, 2)
    tok_step(2, 0)
    carry_in(0)

    arrive(in_q)
    arrive(in_f)

    def attend_fresh(i, carry):
        head = i // 2
        tile = lax.rem(i, 2)
        qt = qb[pl.ds(pl.multiple_of(tile * 256, 256), 256), pl.ds(pl.multiple_of(head * 128, 128), 128)]
        s = dot(qt, fb[:, 0:128], BT)
        allowed = lax.broadcasted_iota(jnp.int32, (256, 512), 1) <= (
            lax.broadcasted_iota(jnp.int32, (256, 512), 0) + tile * 256
        )
        s = jnp.where(allowed, s, LOW)
        top = jnp.max(s, axis=1, keepdims=True)
        w = jnp.exp2((s - top) * SCALE)
        m_s[i] = jnp.broadcast_to(top, (256, 128))
        l_s[i] = jnp.broadcast_to(jnp.sum(w, axis=1, keepdims=True), (256, 128))
        acc_s[i] = dot(w.astype(BF16), fb[:, 128:256])
        return carry

    lax.fori_loop(0, 8, attend_fresh, 0)

    def attend_cached(j):
        owner = y_of(-j)
        if j > 0:
            for k in range(8):
                kv_copies[k, j].wait_recv()

        def tile_of(i, carry):
            head = i // 2
            tile = lax.rem(i, 2)
            qt = qb[
                pl.ds(pl.multiple_of(tile * 256, 256), 256), pl.ds(pl.multiple_of(head * 128, 128), 128)
            ]
            block = kvb[owner].reshape(1024, 256)
            s = dot(qt, block[:, 0:128], BT) + bias[owner]
            old = m_s[i][:, 0:1]
            top = jnp.maximum(old, jnp.max(s, axis=1, keepdims=True))
            w = jnp.exp2((s - top) * SCALE)
            fade = jnp.exp2((old - top) * SCALE)
            m_s[i] = jnp.broadcast_to(top, (256, 128))
            l_s[i] = l_s[i] * fade + jnp.sum(w, axis=1, keepdims=True)
            acc_s[i] = acc_s[i] * fade + dot(w.astype(BF16), block[:, 128:256])
            return carry

        lax.fori_loop(0, 8, tile_of, 0)

    attend_cached(0)
    tok_step(1, 3)
    tok_step(2, 1)
    attend_cached(1)
    tok_step(1, 4)
    tok_step(2, 2)
    tok_step(3, 0)
    carry_in(1)
    attend_cached(2)
    tok_step(2, 3)
    tok_step(3, 1)
    attend_cached(3)

    def finish(i, carry):
        head = i // 2
        tile = lax.rem(i, 2)
        alive = lax.broadcasted_iota(jnp.int32, (256, 128), 0) + tile * 256 < live
        value = jnp.where(alive, acc_s[i] / l_s[i], 0.0)
        ao[
            pl.ds(pl.multiple_of(tile * 256, 256), 256), pl.ds(pl.multiple_of(head * 128, 128), 128)
        ] = value.astype(BF16)
        return carry

    lax.fori_loop(0, 8, finish, 0)
    my_cols = pl.ds(pl.multiple_of(p * 512, 512), 512)
    attn_sends = []
    for d in range(1, NT):
        to = tp_of(d)
        attn_sends.append(
            start(
                remote(
                    ao.at[pl.ds(pl.multiple_of(to * ROWS, ROWS), ROWS), :],
                    attn_out.at[:, my_cols],
                    aos.at[d - 1],
                    aor.at[d - 1],
                    (r, to),
                )
            )
        )
    own_attn = start_local(ao.at[my_rows, :], attn_out.at[:, my_cols])

    tok_step(2, 4)
    tok_step(3, 2)
    carry_in(2)
    tok_step(3, 3)
    tok_step(3, 4)
    carry_in(3)

    in_gate.wait()
    arrive(in_gain)
    for c in range(CHUNKS):
        wait_out(ssm_sends[c])

    def norm(g, carry):
        rows = pl.ds(pl.multiple_of(g * ROWS, ROWS), ROWS)
        parts = []
        square = jnp.zeros((ROWS, 1), F32)
        for c in range(CHUNKS):
            cols = pl.ds(pl.multiple_of(g * 1024 + c * 256, 256), 256)
            gv = gateb[:, cols].astype(F32)
            gated = ob[c, rows, :].astype(F32) * (gv / (1.0 + jnp.exp(-gv)))
            parts.append(gated)
            square = square + jnp.sum(gated * gated, axis=1, keepdims=True)
        factor = lax.rsqrt(square * (1.0 / 1024) + 1e-5)
        alive = lax.broadcasted_iota(jnp.int32, (ROWS, 1), 0) + p * ROWS < live
        factor = jnp.where(alive, factor, 0.0)
        gains = gainb[g]
        for c in range(CHUNKS):
            for e in range(2):
                k = c * 2 + e
                ssm_out[:, pl.ds(pl.multiple_of(g * 1024 + k * 128, 128), 128)] = (
                    parts[c][:, e * 128 : (e + 1) * 128] * factor * gains[k : k + 1, :]
                ).astype(BF16)
        return carry

    lax.fori_loop(0, NT, norm, 0)

    own_attn.wait()
    for copy in attn_sends:
        copy.wait_recv()
    for copy in pending:
        copy.wait_send()


def run(tab, bias, par, gain, step, proj, xin, query, fresh, gate, pool, state):
    any_ = pl.BlockSpec(memory_space=pl.ANY)
    vmem = pl.BlockSpec(memory_space=pltpu.VMEM)
    smem = pl.BlockSpec(memory_space=pltpu.SMEM)
    dma = pltpu.SemaphoreType.DMA
    return pl.pallas_call(
        kernel,
        out_shape=(
            jax.ShapeDtypeStruct((ROWS, 8192), BF16),
            jax.ShapeDtypeStruct((ROWS, 4096), BF16),
        ),
        in_specs=[smem, vmem, vmem] + [any_] * 9,
        out_specs=(vmem, any_),
        scratch_shapes=[
            pltpu.VMEM((512, 128), BF16),
            pltpu.VMEM((NT, 8, 128), F32),
            pltpu.VMEM((512, 512), BF16),
            pltpu.VMEM((512, 1024), BF16),
            pltpu.VMEM((512, 512), BF16),
            pltpu.VMEM((512, 256), BF16),
            pltpu.VMEM((ROWS, 8192), BF16),
            [pltpu.VMEM((4, 64, 256), BF16)] * 8,
            pltpu.VMEM((8, 3, 2, 64, 256), BF16),
            pltpu.VMEM((NY, 8, 2, 64, 256), BF16),
            [pltpu.VMEM((NY, 256, 256), BF16)] * CHUNKS,
            [pltpu.VMEM((8, 256, 256), BF16)] * CHUNKS,
            [pltpu.VMEM((8, 256, 256), BF16)] * CHUNKS,
            pltpu.VMEM((512, 128), F32),
            pltpu.VMEM((512, 128), F32),
            pltpu.VMEM((256, 128), F32),
            pltpu.VMEM((2, 128, 256), F32),
            pltpu.VMEM((2, 128, 256), F32),
            pltpu.VMEM((2, 256, 256), F32),
            pltpu.VMEM((512, 1024), F32),
            pltpu.VMEM((512, 1024), F32),
            pltpu.VMEM((256, 1024), BF16),
            pltpu.VMEM((CHUNKS, 512, 256), BF16),
            pltpu.VMEM((CHUNKS, 512, 256), BF16),
            pltpu.VMEM((8, 256, 128), F32),
            pltpu.VMEM((8, 256, 128), F32),
            pltpu.VMEM((8, 256, 128), F32),
            pltpu.VMEM((512, 512), BF16),
            dma((16,)),
            dma((6, 7)),
            dma((6, 7)),
            dma((8,)),
            dma((8,)),
            dma((8, 3)),
            dma((8, 3)),
            dma((CHUNKS, 3)),
            dma((CHUNKS, 3)),
            dma((CHUNKS, 8)),
            dma((CHUNKS, 8)),
            dma((CHUNKS, 7)),
            dma((CHUNKS, 7)),
            dma((7,)),
            dma((7,)),
        ],
        compiler_params=pltpu.CompilerParams(
            collective_id=0, has_side_effects=True, vmem_limit_bytes=56 * 2**20
        ),
        name="prefill",
    )(tab, bias, par, gain, step, proj, xin, query, fresh, gate, pool, state)


def per_device(
    ssm_input,
    ssm_gate,
    state_proj,
    step_raw,
    queries,
    fresh_kv,
    block_pool,
    state_pool,
    decay_log,
    step_bias,
    skip_gain,
    norm_gain,
    block_owner,
    block_slot,
    block_count,
    state_entry,
    suffix_len,
):
    r = lax.axis_index("req")
    z = r // NY
    y = r % NY
    owner4 = lax.dynamic_slice(block_owner, (z * NY, 0), (NY, 64))
    slot4 = lax.dynamic_slice(block_slot, (z * NY, 0), (NY, 64))
    count4 = lax.dynamic_slice(block_count, (z * NY,), (NY,))
    place = jnp.arange(64, dtype=jnp.int32)
    code = place[None, :] * 4 + slot4
    dist = jnp.array(DIST, jnp.int32)
    owners = ((z - dist + NZ) % NZ)[:, None] * NY + jnp.arange(NY, dtype=jnp.int32)[None, :]
    named = (owner4[:, None, None, :] == owners[None, :, :, None]) & (
        place[None, :] < count4[:, None]
    )[:, None, None, :]
    first = jnp.min(jnp.where(named, code[:, None, None, :], 1024), axis=-1)
    last = jnp.max(jnp.where(named, code[:, None, None, :], -1), axis=-1)
    slot_first = jnp.where(first < 1024, first & 3, 0)
    slot_last = jnp.where(last >= 0, last & 3, 0)
    live = lax.dynamic_slice(suffix_len, (r,), (1,))
    column = state_entry.reshape(NZ, NY)
    entries = lax.dynamic_slice(column, (0, y), (NZ, 1))[:, 0]
    misc = jnp.concatenate([entries // NY, entries % NY, live, jnp.zeros((111,), jnp.int32)])
    tab = jnp.stack([slot_first.reshape(128), slot_last.reshape(128), misc])
    mine_first = lax.dynamic_index_in_dim(first, y, 0, keepdims=False)
    mine_last = lax.dynamic_index_in_dim(last, y, 0, keepdims=False)
    valid = jnp.stack([mine_first < 1024, mine_last > mine_first], axis=-1)
    bias = jnp.where(valid.transpose(1, 0, 2), 0.0, LOW).astype(F32)
    bias = jnp.repeat(bias.reshape(NY, 1, 16), 64, axis=2)
    par = jnp.stack(
        [
            jnp.repeat(skip_gain, 64),
            jnp.pad(step_bias, (0, 1008)),
            jnp.pad(decay_log, (0, 1008)),
        ]
    )
    ssm, attn = run(
        tab,
        bias,
        par,
        norm_gain.reshape(8, 128),
        step_raw[0],
        state_proj[0],
        ssm_input[0],
        queries[0],
        fresh_kv[0],
        ssm_gate[0],
        block_pool.reshape(4, 64, 256),
        state_pool.reshape(CHUNKS, 256, 256),
    )
    return (ssm[None], attn[None])


def solution(mesh):
    return jax.shard_map(
        per_device,
        mesh=mesh,
        in_specs=(
            P("req", "tp", None),
            P("req", "tp", None),
            P("req", "tp", None),
            P("req", "tp", None),
            P("req", "tp", None),
            P("req", "tp", None),
            P("req", None, "tp", None),
            P("req", "tp", None, None),
            P("tp"),
            P("tp"),
            P("tp"),
            P("tp"),
            P(),
            P(),
            P(),
            P(),
            P(),
        ),
        out_specs=(P("req", "tp", None), P("req", "tp", None)),
        check_vma=False,
    )
```

time: 451 us -> 112 us (0.25); the launches traced: 443 us -> 112 us
  other arithmetic: 186 us -> 3.49 us
  local copies, waits for them, and re-layouts: 140 us -> 9.94 us
  Pallas kernels: 0 us -> 97.3 us
  matrix products: 41.9 us -> 0 us
  starting transfers between devices: 41.6 us -> 0 us
  between operations: 15.6 us -> 0.75 us
  waiting for transfers between devices: 13.3 us -> 0 us
  loops' own time: 4.89 us -> 0 us
    unnamed x9 -> x0, other arithmetic: 159 us -> none
    pallas_call x0 -> x1, Pallas kernels: none -> 97.3 us  [run(): pl.pallas_call(kernel, out_shape=(jax.ShapeDtypeStruct((ROWS, 8192), BF16...]
    unnamed x77 -> x18, local copies, waits for them, and re-layouts: 74 us -> 7.51 us
    dot_general x13 -> x0, matrix products: 41.9 us -> none  [the longest x1 15.8 us: per_device(): jnp.einsum('e,emdn->mdn', marks, shard_rows, preferred_element_type=jnp.f...]
    all_to_all x8 -> x0, starting transfers between devices: 41.5 us -> none  [the longest x1 6.48 us: per_device(): lax.all_to_all(step_raw, 'tp', split_axis=2, concat_axis=1, tiled=True)]
    all_to_all x16 -> x0, local copies, waits for them, and re-layouts: 29.2 us -> none  [the longest x3 9.78 us: per_device(): lax.all_to_all(ssm_input, 'tp', split_axis=2, concat_axis=1, tiled=True)]
    convert_element_type x8 -> x0, local copies, waits for them, and re-layouts: 12.7 us -> none  [the longest x5 10.4 us: scan_heads(): gate_rows.astype(jnp.float32)]
    all_to_all x8 -> x0, waiting for transfers between devices: 11.9 us -> none  [the longest x1 11.9 us: per_device(): lax.all_to_all(mamba[None], 'tp', split_axis=1, concat_axis=2, tiled=True)]
  transfers between devices with their start and end apart: 10 -> 0, of which waited for: 1 -> 0; matrix products, arithmetic and copies ran while one was open for 81% -> 0% of each run, Pallas kernels for 0% -> 0%
where the time goes in v1:
time: 112 us
  Pallas kernels  97.3 us (87%)
  local copies, waits for them, and re-layouts  9.94 us (9%)
  other arithmetic  3.49 us (3%)
    pallas_call x1, Pallas kernels, run(): pl.pallas_call(kernel, out_shape=(jax.ShapeDtypeStruct((ROWS, 8192), BF16...  97.3 us
    unnamed x18, local copies, waits for them, and re-layouts  7.51 us

profile of v1, /device:TPU:1, one launch (start us, length us, event | category | flops | bytes accessed | tf_op | source)
XLA Modules:
  0.0 111.5 jit_solution(1563179584712455873)
XLA Ops:
  0.7 0.0 copy-start.6
  0.7 0.6 copy-done.6
  1.3 0.6 dynamic_slice.26
  1.9 0.0 copy-start.7
  1.9 0.7 copy-done.7
  2.6 0.1 dynamic_slice.23
  2.6 0.1 iota_compare_fusion
  2.7 0.7 dynamic-slice_add_fusion
  3.4 0.0 copy-start.1
  3.4 0.7 copy-done.1
  4.1 0.0 copy-start.2
  4.1 0.7 copy-done.2
  4.7 0.0 copy-start.3
  4.7 0.7 copy-done.3
  5.4 0.1 reshape.157
  5.5 0.0 copy-start.5
  5.5 0.2 dynamic-slice_reduce_fusion
  5.7 0.5 copy-done.5
  6.2 0.7 add_bitcast_fusion
  6.9 0.0 copy-start.4
  6.9 0.7 copy-done.4
  7.5 0.1 broadcast_in_dim.67
  7.6 0.1 stack_reshape.2
  7.7 0.6 pad_maximum_fusion.par
  8.3 0.7 select_reduce_fusion.1
  9.1 0.1 copy.30
  9.2 0.1 copy.31
  9.3 0.1 copy.28
  9.4 0.1 select_n.86
  9.5 0.1 copy.29
  9.6 0.1 select_n.89
  9.7 0.6 pad_add_fusion.tab
  10.3 0.1 broadcast_in_dim.65
  10.3 0.7 broadcast_in_dim.66.bias
  11.0 97.3 %prefill.1 = (bf16[64,8192]{1,0:T(8,128)(2,1)}, bf16[64,4096]{1,0:T(8,128)(2,1)}) custom-call(s32[3,128]{1,0:T(4,128)} %pad_add_fusion.tab, f32[4,1,1024]{2,1,0:T(1,128)} %broadcast_in_dim.66.bias, f32[3,1024]{1,0:T(4,128)} %pad_maximum_fusion.par, f32[8,128]{1,0:T(8,128)} %bitcast.35, bf16[64,128]{1,0:T(8,128)(2,1)} %bitcast.32, bf16[64,4096]{1,0:T(8,128)(2,1)} %bitcast.25, ...), custom_call_target="tpu_custom_call" | custom-call | tf_op jit(solution)/shard_map/prefill/pallas_call | solution.py:519
  108.4 0.0 copy-start
  108.4 2.3 %copy.34 = bf16[1,64,8192]{2,1,0:T(8,128)(2,1)} copy(bf16[1,64,8192]{2,1,0:T(8,128)(2,1)} %bitcast.24) | data formatting | bytes 2097152
  110.7 0.0 copy-done
  110.7 0.8 copy.35
  (10 shorter events, 0.1 us)
Async XLA Ops:
  0.7 0.7 copy-start.6
  1.9 0.7 copy-start.7
  3.4 0.7 copy-start.1
  4.1 0.7 copy-start.2
  4.7 0.7 copy-start.3
  5.5 0.7 copy-start.5
  6.9 0.7 copy-start.4
  108.4 2.3 %copy-start = (bf16[64,4096]{1,0:T(8,128)(2,1)S(1)}, bf16[64,4096]{1,0:T(8,128)(2,1)}, u32[]{:S(2)}) copy-start(bf16[64,4096]{1,0:T(8,128)(2,1)} %get-tuple-element.5) | copy-start | bytes 1572868

commit v2 on v1

v2 whole, which is shorter than its diff:
```python
import jax
import jax.numpy as jnp
from jax import lax
from jax.experimental import pallas as pl
from jax.experimental.pallas import tpu as pltpu
from jax.sharding import PartitionSpec as P

MESH = pl.DeviceIdType.MESH
F32 = jnp.float32
BF16 = jnp.bfloat16

NZ, NY, NT = 8, 4, 8
ROWS = 64
SPAN = 256
PARTS = 8
FLIGHT = 4
DIST = (0, 1, -1, 2, -2, 3, -3, 4)
LOW = -1e30
SCALE = 1.4426950408889634 / 128**0.5


def dot(a, b, dims=(((1,), (0,)), ((), ())), precision=None):
    return lax.dot_general(a, b, dims, precision=precision, preferred_element_type=F32)


BT = (((1,), (1,)), ((), ()))
AT = (((0,), (0,)), ((), ()))


def kernel(
    owner_in,
    slot_in,
    count_in,
    entry_in,
    suffix_in,
    decay_in,
    bias_in,
    skip_in,
    gain,
    step,
    proj,
    xin,
    query,
    fresh,
    gate,
    pool,
    state,
    ssm_out,
    attn_out,
    owner,
    slot,
    count,
    entry,
    suffix,
    decay_log,
    step_bias,
    skip_gain,
    tabv,
    tabs,
    bias,
    stepb,
    gainb,
    projb,
    xb,
    qb,
    fb,
    gateb,
    gact,
    add_s,
    kz,
    ksend,
    kvb,
    yb,
    tk,
    ts,
    cum_c,
    w_c,
    cum_r,
    dt_r,
    inner,
    yint,
    ecx,
    tailb,
    osend,
    ob,
    m_s,
    l_s,
    acc_s,
    ao,
    tsem,
    lsem,
    xs,
    xr,
    kzs,
    kzr,
    kys,
    kyr,
    sys_,
    syr,
    tss,
    tsr,
    oss,
    osr,
    aos,
    aor,
):
    r = lax.axis_index("req")
    p = lax.axis_index("tp")
    z = r // NY
    y = lax.rem(r, NY)

    def tp_of(d):
        return lax.rem(p + d, NT)

    def z_of(k):
        return lax.rem(z + k + 2 * NZ, NZ)

    def y_of(k):
        return lax.rem(y + k + NY, NY)

    def remote(src, dst, ssem, rsem, device):
        return pltpu.make_async_remote_copy(
            src_ref=src, dst_ref=dst, send_sem=ssem, recv_sem=rsem, device_id=device, device_id_type=MESH
        )

    small = [
        pltpu.make_async_copy(src, dst, tsem.at[1 + i])
        for i, (src, dst) in enumerate(
            (
                (owner_in, owner),
                (slot_in, slot),
                (count_in, count),
                (entry_in, entry),
                (suffix_in, suffix),
                (decay_in, decay_log),
                (bias_in, step_bias),
                (skip_in, skip_gain),
            )
        )
    ]
    for copy in small:
        copy.start()

    barrier = pltpu.get_barrier_semaphore()
    peers = [(r, tp_of(d)) for d in range(1, NT)]
    peers += [(z_of(1) * NY + y, p), (z_of(-1) * NY + y, p)]
    peers += [(z * NY + y_of(j), p) for j in range(1, NY)]
    for peer in peers:
        pl.semaphore_signal(barrier, inc=1, device_id=peer, device_id_type=MESH)

    pending = []
    local = []

    def start(copy):
        copy.start()
        pending.append(copy)
        return copy

    def start_local(src, dst):
        copy = pltpu.make_async_copy(src, dst, lsem.at[len(local)])
        copy.start()
        local.append(copy)
        return copy

    my_rows = pl.ds(pl.multiple_of(p * ROWS, ROWS), ROWS)
    own_pool = start_local(pool, kz[0])

    pl.semaphore_wait(barrier, len(peers))

    def spread(i, src, dst, width):
        out = [start_local(src.at[:, pl.ds(pl.multiple_of(p * width, 128), width)], dst.at[my_rows, :])]
        for d in range(1, NT):
            to = tp_of(d)
            out.append(
                start(
                    remote(
                        src.at[:, pl.ds(pl.multiple_of(to * width, 128), width)],
                        dst.at[my_rows, :],
                        xs.at[i, d - 1],
                        xr.at[i, d - 1],
                        (r, to),
                    )
                )
            )
        return out

    def everyone(i, src, dst):
        out = [start_local(src, dst)]
        for d in range(1, NT):
            out.append(start(remote(src, dst, xs.at[i, d - 1], xr.at[i, d - 1], (r, tp_of(d)))))
        return out

    def arrive(copies):
        copies[0].wait()
        for copy in copies[1:]:
            copy.wait_recv()

    gathers = {}

    def gather_state(c):
        out = [start_local(state.at[c], yb[c].at[y])]
        for j in range(1, NY):
            out.append(
                start(
                    remote(
                        state.at[c],
                        yb[c].at[y],
                        sys_.at[c, j - 1],
                        syr.at[c, j - 1],
                        (z * NY + y_of(j), p),
                    )
                )
            )
        gathers[c] = out

    def length(parity, way):
        return 4 if (way > 0) == (parity == 0) else 3

    hops = {}

    def kv_slot(s, way):
        return DIST.index(s * way) if s < 4 else 7

    def kv_hop(f, s, way):
        slot_now = kv_slot(s, way)
        part = pl.ds(2 * f, 2)
        before = pool if s == 1 else kz[kv_slot(s - 1, way)]
        place = slot_now
        hops[f, s, way] = start(
            remote(
                before.at[part],
                kz[place].at[part],
                kzs.at[f, place],
                kzr.at[f, place],
                (z_of(way) * NY + y, p),
            )
        )

    kv_copies = {}

    def kv_across(k):
        source = lax.rem(z - DIST[k] + NZ, NZ) * NY + y
        for j in range(NY):
            to = y_of(j)
            word = tabs[source, to]
            first = kz[k][lax.rem(word, 4)]
            second = kz[k][lax.rem(lax.div(word, 4), 4)]
            if j == 0:
                kvb[k, y, 0] = first
                kvb[k, y, 1] = second
            else:
                ksend[k, j - 1, 0] = first
                ksend[k, j - 1, 1] = second
                kv_copies[k, j] = start(
                    remote(
                        ksend.at[k, j - 1],
                        kvb.at[k, y],
                        kys.at[k, j - 1],
                        kyr.at[k, j - 1],
                        (z * NY + to, p),
                    )
                )

    def kv_step(f, s):
        for way in (1, -1):
            if s <= length(f, way):
                hops[f, s, way].wait_recv()
                if s < length(f, way):
                    kv_hop(f, s + 1, way)
        if f == 1:
            if s < 4:
                kv_across(DIST.index(s))
                kv_across(DIST.index(-s))
            else:
                kv_across(7)

    tokens = {}

    def tok_hop(c, s, way):
        total = length(c % 2, way)
        dest = z_of(way * (total - s + 1))
        base = 0 if way > 0 else 4
        e = entry[dest * NY + y]
        mine = yb[c][lax.rem(e, NY)]
        if s > 1:
            mine = jnp.where(lax.div(e, NY) == z, mine, tk[c][base + s - 2])
        ts[c][base + s - 1] = mine
        tokens[c, s, way] = start(
            remote(
                ts[c].at[base + s - 1],
                tk[c].at[base + s - 1],
                tss.at[c, base + s - 1],
                tsr.at[c, base + s - 1],
                (z_of(way) * NY + y, p),
            )
        )

    def tok_start(c):
        arrive(gathers[c])
        tok_hop(c, 1, 1)
        tok_hop(c, 1, -1)

    def tok_step(c, s):
        for way in (1, -1):
            if s <= length(c % 2, way):
                tokens[c, s, way].wait_recv()
                if s < length(c % 2, way):
                    tok_hop(c, s + 1, way)

    for f in range(2):
        kv_hop(f, 1, 1)
        kv_hop(f, 1, -1)
    gather_state(0)
    gather_state(1)
    in_step = everyone(0, step, stepb.at[my_rows, :])
    in_proj = spread(1, proj, projb, 512)
    in_x = spread(2, xin, xb, 1024)
    for c in range(2, PARTS):
        gather_state(c)
    in_q = spread(3, query, qb, 512)
    in_f = spread(4, fresh, fb, 256)
    in_gain = everyone(5, gain, gainb.at[p])
    in_gate = start_local(gate, gateb)

    for copy in small:
        copy.wait()
    lane = lax.broadcasted_iota(jnp.int32, (NZ * NY, 64), 1)
    who = lax.broadcasted_iota(jnp.int32, (NZ * NY, 64), 0)
    wide = lax.broadcasted_iota(jnp.int32, (NZ * NY, 128), 1)
    packed = jnp.zeros((NZ * NY, 128), jnp.int32)
    for t in range(NY):
        row = pl.ds(z * NY + t, 1)
        named = (owner[row, :] == who) & (lane < count[z * NY + t])
        code = lane * 4 + slot[row, :]
        first = jnp.min(jnp.where(named, code, 1024), axis=1, keepdims=True)
        last = jnp.max(jnp.where(named, code, -1), axis=1, keepdims=True)
        value = (
            (first & 3)
            + 4 * (last & 3)
            + jnp.where(first < 1024, 16, 0)
            + jnp.where(last > first, 32, 0)
        )
        packed = jnp.where(wide == t, value, packed)
    tabv[...] = packed
    to_scalars = pltpu.make_async_copy(tabv, tabs, tsem.at[0])
    to_scalars.start()

    to_scalars.wait()
    own_pool.wait()
    kv_across(0)
    live = suffix[r]

    side = lax.broadcasted_iota(jnp.int32, (1, 128), 1)
    for k in range(8):
        for t in range(NY):
            word = tabs[lax.rem(z - DIST[k] + NZ, NZ) * NY + t, y]
            flag = jnp.where(side < 64, lax.rem(lax.div(word, 16), 2), lax.div(word, 32))
            place = (k % 2) * 512 + t * 128
            bias[k // 2, :, place : place + 128] = jnp.where(flag > 0, 0.0, LOW)

    lower = lax.broadcasted_iota(jnp.int32, (SPAN, SPAN), 0) >= lax.broadcasted_iota(
        jnp.int32, (SPAN, SPAN), 1
    )
    half = lax.broadcasted_iota(jnp.int32, (SPAN, 128), 1) < 64

    def scan_sums():
        arrive(in_step)
        take = (
            lax.broadcasted_iota(jnp.int32, (128, 128), 0)
            == lax.broadcasted_iota(jnp.int32, (128, 128), 1) + p * 16
        ).astype(BF16)
        shift = jnp.zeros((1, 128), F32)
        rate = jnp.zeros((1, 128), F32)
        for h in range(16):
            shift = jnp.where(side == h, step_bias[h], shift)
            rate = jnp.where(side == h, decay_log[h], rate)
        raw = dot(stepb[...], take) + shift
        dt = jnp.maximum(raw, 0.0) + jnp.log1p(jnp.exp(-jnp.abs(raw)))
        drop = dt * -jnp.exp(rate)
        ones = lower.astype(F32)
        for b in range(2):
            rows = slice(b * SPAN, (b + 1) * SPAN)
            cum = dot(ones, drop[rows], precision=lax.Precision.HIGHEST)
            cum_c[rows, :] = cum
            cum_r[b] = cum.T
            dt_r[b] = dt[rows].T
            if b == 0:
                w_c[...] = jnp.exp(cum[SPAN - 1 : SPAN] - cum) * dt[rows]

    def scan_inner():
        arrive(in_proj)
        for b in range(2):
            rows = slice(b * SPAN, (b + 1) * SPAN)
            inner[b] = dot(projb[rows, 256:512], projb[rows, 0:256], BT)
        arrive(in_x)

    def pair(hp, carry):
        cols = pl.ds(pl.multiple_of(hp * 128, 128), 128)
        skip = jnp.where(half, skip_gain[hp * 2], skip_gain[hp * 2 + 1])
        for b in range(2):
            rows = slice(b * SPAN, (b + 1) * SPAN)
            xp = xb[rows, cols]
            cum_b = cum_c[rows, :]
            res, cumcols, weights = [], [], []
            for e in range(2):
                h = hp * 2 + e
                column = pltpu.roll(cum_b, 128 - h, 1)[:, 0:1]
                spread_cum = column - cum_r[b, pl.ds(h, 1), :]
                mix = jnp.exp(jnp.where(lower, spread_cum, LOW)) * inner[b] * dt_r[b, pl.ds(h, 1), :]
                res.append(dot(mix.astype(BF16), xp))
                cumcols.append(column)
                if b == 0:
                    weights.append(pltpu.roll(w_c[...], 128 - h, 1)[:, 0:1])
            xf = xp.astype(F32)
            ecx[rows, cols] = jnp.exp(jnp.where(half, cumcols[0], cumcols[1]))
            yint[rows, cols] = jnp.where(half, res[0], res[1]) + skip * xf
            if b == 0:
                tailb[:, cols] = (jnp.where(half, weights[0], weights[1]) * xf).astype(BF16)
        return carry

    def scan_add():
        add_s[...] = dot(projb[0:SPAN, 0:256], tailb[...], AT)

    def open_gate():
        in_gate.wait()

        def some(g, carry):
            cols = pl.ds(pl.multiple_of(g * 1024, 1024), 1024)
            gv = gateb[:, cols].astype(F32)
            gact[:, cols] = gv / (1.0 + jnp.exp(-gv))
            return carry

        lax.fori_loop(0, NT, some, 0)

    ssm_sends = []

    def carry_in(lo, hi):
        e = entry[r]
        ze = lax.div(e, NY)
        behind = lax.rem(z - ze + NZ, NZ)
        eye = (
            lax.broadcasted_iota(jnp.int32, (256, 256), 0) == lax.broadcasted_iota(jnp.int32, (256, 256), 1)
        ).astype(BF16)
        for c in range(lo, hi):
            ahead, back = length(c % 2, 1), length(c % 2, -1)
            entering = jnp.where(behind <= ahead, tk[c][ahead - 1], tk[c][4 + back - 1])
            s0 = jnp.where(ze == z, yb[c][lax.rem(e, NY)], entering)
            cols = slice(c * 128, (c + 1) * 128)
            s0t = dot(eye, s0, BT)
            s1t = ecx[SPAN - 1 : SPAN, cols] * s0t + add_s[:, cols]
            for b, st in ((0, s0t), (1, s1t)):
                rows = slice(b * SPAN, (b + 1) * SPAN)
                carried = dot(projb[rows, 256:512], st.astype(BF16))
                osend[rows, cols] = (yint[rows, cols] + ecx[rows, cols] * carried).astype(BF16)
        cols = slice(lo * 128, hi * 128)
        for d in range(1, NT):
            to = tp_of(d)
            ssm_sends.append(
                start(
                    remote(
                        osend.at[pl.ds(pl.multiple_of(to * ROWS, ROWS), ROWS), cols],
                        ob.at[my_rows, cols],
                        oss.at[lo, d - 1],
                        osr.at[lo, d - 1],
                        (r, to),
                    )
                )
            )
        ob[my_rows, cols] = osend[my_rows, cols]

    def attend_fresh(i, carry):
        head = i // 2
        tile = lax.rem(i, 2)
        qt = qb[pl.ds(pl.multiple_of(tile * 256, 256), 256), pl.ds(pl.multiple_of(head * 128, 128), 128)]
        s = dot(qt, fb[:, 0:128], BT)
        allowed = lax.broadcasted_iota(jnp.int32, (256, 512), 1) <= (
            lax.broadcasted_iota(jnp.int32, (256, 512), 0) + tile * 256
        )
        s = jnp.where(allowed, s, LOW)
        top = jnp.max(s, axis=1, keepdims=True)
        w = jnp.exp2((s - top) * SCALE)
        m_s[i] = jnp.broadcast_to(top, (256, 128))
        l_s[i] = jnp.broadcast_to(jnp.sum(w, axis=1, keepdims=True), (256, 128))
        acc_s[i] = dot(w.astype(BF16), fb[:, 128:256])
        return carry

    def attend_first():
        arrive(in_q)
        arrive(in_f)
        lax.fori_loop(0, 8, attend_fresh, 0)

    def attend_cached(n, lo, hi):
        if lo == 0:
            for k in (2 * n, 2 * n + 1):
                for j in range(1, NY):
                    kv_copies[k, j].wait_recv()

        def tile_of(i, carry):
            head = i // 2
            tile = lax.rem(i, 2)
            qt = qb[
                pl.ds(pl.multiple_of(tile * 256, 256), 256), pl.ds(pl.multiple_of(head * 128, 128), 128)
            ]
            block = kvb[2 * n : 2 * n + 2].reshape(1024, 256)
            s = dot(qt, block[:, 0:128], BT) + bias[n]
            old = m_s[i][:, 0:1]
            top = jnp.maximum(old, jnp.max(s, axis=1, keepdims=True))
            w = jnp.exp2((s - top) * SCALE)
            fade = jnp.exp2((old - top) * SCALE)
            m_s[i] = jnp.broadcast_to(top, (256, 128))
            l_s[i] = l_s[i] * fade + jnp.sum(w, axis=1, keepdims=True)
            acc_s[i] = acc_s[i] * fade + dot(w.astype(BF16), block[:, 128:256])
            return carry

        lax.fori_loop(lo, hi, tile_of, 0)

    my_cols = pl.ds(pl.multiple_of(p * 512, 512), 512)
    attn_sends = []
    own_attn = []

    def finish(i, carry):
        head = i // 2
        tile = lax.rem(i, 2)
        alive = lax.broadcasted_iota(jnp.int32, (256, 128), 0) + tile * 256 < live
        value = jnp.where(alive, acc_s[i] / l_s[i], 0.0)
        ao[
            pl.ds(pl.multiple_of(tile * 256, 256), 256), pl.ds(pl.multiple_of(head * 128, 128), 128)
        ] = value.astype(BF16)
        return carry

    def attend_last():
        lax.fori_loop(0, 8, finish, 0)
        for d in range(1, NT):
            to = tp_of(d)
            attn_sends.append(
                start(
                    remote(
                        ao.at[pl.ds(pl.multiple_of(to * ROWS, ROWS), ROWS), :],
                        attn_out.at[:, my_cols],
                        aos.at[d - 1],
                        aor.at[d - 1],
                        (r, to),
                    )
                )
            )
        own_attn.append(start_local(ao.at[my_rows, :], attn_out.at[:, my_cols]))

    waiting = [("kv", 0), ("kv", 1)] + [("st", c) for c in range(PARTS)]
    under_way = []
    ended = []
    work = list(WORK)
    done = set()
    count_rounds = 0
    marks = []

    def do(item):
        name, args = item[1], item[2:]
        if name == "sums":
            scan_sums()
        elif name == "inner":
            scan_inner()
        elif name == "pair":
            lax.fori_loop(args[0], args[1], pair, 0)
        elif name == "carry":
            carry_in(*args)
        elif name == "fresh":
            attend_first()
        elif name == "cached":
            attend_cached(*args)
        elif name == "finish":
            attend_last()
        elif name == "add":
            scan_add()
        elif name == "gate":
            open_gate()
        elif name == "gain":
            arrive(in_gain)
        elif name == "drain":
            while pending[0] is not marks[args[0]]:
                pending.pop(0).wait_send()

    def able(item):
        if item[1] == "carry":
            return all(c in done for c in range(item[2], item[3]))
        return item[0] <= count_rounds

    while waiting or under_way:
        for one in list(under_way):
            kind, n, s = one
            (kv_step if kind == "kv" else tok_step)(n, s)
            if s == 4:
                under_way.remove(one)
                if kind == "st":
                    done.add(n)
            else:
                under_way[under_way.index(one)] = (kind, n, s + 1)
        room = 2 if count_rounds < 1 else 1
        while waiting and len(under_way) < FLIGHT and room > 0:
            room -= 1
            kind, n = waiting.pop(0)
            if kind == "st":
                tok_start(n)
            under_way.append((kind, n, 1))
        count_rounds += 1
        marks.append(pending[-1])
        budget = BUDGET
        for item in list(work):
            if budget > 0 and able(item):
                work.remove(item)
                do(item)
                budget -= COST[item[1]]
    for item in list(work):
        do(item)

    for copy in ssm_sends:
        copy.wait_recv()

    def norm(g, carry):
        rows = pl.ds(pl.multiple_of(g * ROWS, ROWS), ROWS)
        parts = []
        square = jnp.zeros((ROWS, 1), F32)
        for c in range(4):
            act = gact[:, pl.ds(pl.multiple_of(g * 1024 + c * 256, 256), 256)]
            gated = ob[rows, c * 256 : (c + 1) * 256].astype(F32) * act
            parts.append(gated)
            square = square + jnp.sum(gated * gated, axis=1, keepdims=True)
        factor = lax.rsqrt(square * (1.0 / 1024) + 1e-5)
        alive = lax.broadcasted_iota(jnp.int32, (ROWS, 1), 0) + p * ROWS < live
        factor = jnp.where(alive, factor, 0.0)
        gains = gainb[g]
        for c in range(4):
            for e in range(2):
                k = c * 2 + e
                ssm_out[:, pl.ds(pl.multiple_of(g * 1024 + k * 128, 128), 128)] = (
                    parts[c][:, e * 128 : (e + 1) * 128] * factor * gains[k : k + 1, :]
                ).astype(BF16)
        return carry

    lax.fori_loop(0, NT, norm, 0)

    own_attn[0].wait()
    for copy in attn_sends:
        copy.wait_recv()
    for copy in pending:
        copy.wait_send()


BUDGET = 3.5
COST = {
    "sums": 1.0,
    "inner": 0.5,
    "pair": 1.5,
    "add": 0.6,
    "carry": 1.2,
    "fresh": 4.0,
    "cached": 1.6,
    "finish": 1.0,
    "gate": 1.2,
    "gain": 0.1,
    "drain": 0.3,
}
WORK = (
    (3, "sums"),
    (3, "gate"),
    (4, "inner"),
    (4, "pair", 0, 2),
    (4, "pair", 2, 4),
    (5, "pair", 4, 6),
    (5, "pair", 6, 8),
    (5, "add"),
    (6, "carry", 0, 2),
    (6, "gain"),
    (6, "fresh"),
    (6, "carry", 2, 4),
    (7, "drain", 1),
    (7, "cached", 0, 0, 2),
    (7, "cached", 0, 2, 4),
    (7, "cached", 0, 4, 6),
    (7, "cached", 0, 6, 8),
    (8, "carry", 4, 6),
    (8, "cached", 1, 0, 2),
    (8, "cached", 1, 2, 4),
    (8, "cached", 1, 4, 6),
    (8, "cached", 1, 6, 8),
    (9, "drain", 4),
    (9, "cached", 2, 0, 2),
    (9, "cached", 2, 2, 4),
    (9, "cached", 2, 4, 6),
    (9, "cached", 2, 6, 8),
    (10, "cached", 3, 0, 2),
    (10, "cached", 3, 2, 4),
    (10, "cached", 3, 4, 6),
    (10, "cached", 3, 6, 8),
    (10, "finish"),
    (11, "drain", 8),
    (12, "carry", 6, 7),
    (12, "carry", 7, 8),
)


def run(*args):
    any_ = pl.BlockSpec(memory_space=pl.ANY)
    vmem = pl.BlockSpec(memory_space=pltpu.VMEM)
    dma = pltpu.SemaphoreType.DMA
    return pl.pallas_call(
        kernel,
        out_shape=(
            jax.ShapeDtypeStruct((ROWS, 8192), BF16),
            jax.ShapeDtypeStruct((ROWS, 4096), BF16),
        ),
        in_specs=[any_] * 17,
        out_specs=(vmem, any_),
        scratch_shapes=[
            pltpu.VMEM((NZ * NY, 64), jnp.int32),
            pltpu.VMEM((NZ * NY, 64), jnp.int32),
            pltpu.SMEM((NZ * NY,), jnp.int32),
            pltpu.SMEM((NZ * NY,), jnp.int32),
            pltpu.SMEM((NZ * NY,), jnp.int32),
            pltpu.SMEM((16,), F32),
            pltpu.SMEM((16,), F32),
            pltpu.SMEM((16,), F32),
            pltpu.VMEM((NZ * NY, 128), jnp.int32),
            pltpu.SMEM((NZ * NY, 128), jnp.int32),
            pltpu.VMEM((4, 1, 1024), F32),
            pltpu.VMEM((512, 128), BF16),
            pltpu.VMEM((NT, 8, 128), F32),
            pltpu.VMEM((512, 512), BF16),
            pltpu.VMEM((512, 1024), BF16),
            pltpu.VMEM((512, 512), BF16),
            pltpu.VMEM((512, 256), BF16),
            pltpu.VMEM((ROWS, 8192), BF16),
            pltpu.VMEM((ROWS, 8192), F32),
            pltpu.VMEM((256, 1024), F32),
            [pltpu.VMEM((4, 64, 256), BF16)] * 8,
            pltpu.VMEM((8, 3, 2, 64, 256), BF16),
            pltpu.VMEM((8, NY, 2, 64, 256), BF16),
            [pltpu.VMEM((NY, 128, 256), BF16)] * PARTS,
            [pltpu.VMEM((8, 128, 256), BF16)] * PARTS,
            [pltpu.VMEM((8, 128, 256), BF16)] * PARTS,
            pltpu.VMEM((512, 128), F32),
            pltpu.VMEM((256, 128), F32),
            pltpu.VMEM((2, 128, 256), F32),
            pltpu.VMEM((2, 128, 256), F32),
            pltpu.VMEM((2, 256, 256), F32),
            pltpu.VMEM((512, 1024), F32),
            pltpu.VMEM((512, 1024), F32),
            pltpu.VMEM((256, 1024), BF16),
            pltpu.VMEM((512, 1024), BF16),
            pltpu.VMEM((512, 1024), BF16),
            pltpu.VMEM((8, 256, 128), F32),
            pltpu.VMEM((8, 256, 128), F32),
            pltpu.VMEM((8, 256, 128), F32),
            pltpu.VMEM((512, 512), BF16),
            dma((9,)),
            dma((24,)),
            dma((6, 7)),
            dma((6, 7)),
            dma((2, 8)),
            dma((2, 8)),
            dma((8, 3)),
            dma((8, 3)),
            dma((PARTS, 3)),
            dma((PARTS, 3)),
            dma((PARTS, 8)),
            dma((PARTS, 8)),
            dma((PARTS, 7)),
            dma((PARTS, 7)),
            dma((7,)),
            dma((7,)),
        ],
        compiler_params=pltpu.CompilerParams(
            collective_id=0, has_side_effects=True, vmem_limit_bytes=56 * 2**20
        ),
        name="prefill",
    )(*args)


def per_device(
    ssm_input,
    ssm_gate,
    state_proj,
    step_raw,
    queries,
    fresh_kv,
    block_pool,
    state_pool,
    decay_log,
    step_bias,
    skip_gain,
    norm_gain,
    block_owner,
    block_slot,
    block_count,
    state_entry,
    suffix_len,
):
    ssm, attn = run(
        block_owner,
        block_slot,
        block_count,
        state_entry,
        suffix_len,
        decay_log,
        step_bias,
        skip_gain,
        norm_gain.reshape(8, 128),
        step_raw[0],
        state_proj[0],
        ssm_input[0],
        queries[0],
        fresh_kv[0],
        ssm_gate[0],
        block_pool.reshape(4, 64, 256),
        state_pool.reshape(PARTS, 128, 256),
    )
    return (ssm[None], attn[None])


def solution(mesh):
    return jax.shard_map(
        per_device,
        mesh=mesh,
        in_specs=(
            P("req", "tp", None),
            P("req", "tp", None),
            P("req", "tp", None),
            P("req", "tp", None),
            P("req", "tp", None),
            P("req", "tp", None),
            P("req", None, "tp", None),
            P("req", "tp", None, None),
            P("tp"),
            P("tp"),
            P("tp"),
            P("tp"),
            P(),
            P(),
            P(),
            P(),
            P(),
        ),
        out_specs=(P("req", "tp", None), P("req", "tp", None)),
        check_vma=False,
    )
```

time: 112 us -> 99.9 us (0.89)
  local copies, waits for them, and re-layouts: 9.94 us -> 3.12 us
  other arithmetic: 3.49 us -> 0 us
  Pallas kernels: 97.3 us -> 96.1 us
    unnamed x18 -> x4, local copies, waits for them, and re-layouts: 7.51 us -> 3.12 us
    another operation x3 -> x0, other arithmetic: 1.95 us -> none  [the longest x2 1.33 us: per_device(): tab = jnp.stack([slot_first.reshape(128), slot_last.reshape(128), misc])]
    pallas_call x1, Pallas kernels: 97.3 us -> 96.1 us  [run(): pl.pallas_call(kernel, out_shape=(jax.ShapeDtypeStruct((ROWS, 8192), BF16...]
where the time goes in v2:
time: 99.9 us; the launch traced here: 99.8 us
  Pallas kernels  96.1 us (96%)
  local copies, waits for them, and re-layouts  3.12 us (3%)
    pallas_call x1, Pallas kernels, run(): pl.pallas_call(kernel, out_shape=(jax.ShapeDtypeStruct((ROWS, 8192), BF16...  96.1 us
    unnamed x4, local copies, waits for them, and re-layouts  3.12 us

profile of v2, /device:TPU:1, one launch (start us, length us, event | category | flops | bytes accessed | tf_op | source)
XLA Modules:
  0.0 99.8 jit_solution(3285696147466615402)
XLA Ops:
  0.6 96.1 %prefill.1 = (bf16[64,8192]{1,0:T(8,128)(2,1)}, bf16[64,4096]{1,0:T(8,128)(2,1)}) custom-call(s32[32,64]{1,0:T(8,128)} %owner_in.1, s32[32,64]{1,0:T(8,128)} %slot_in.1, s32[32]{0:T(128)} %count_in.1, s32[32]{0:T(128)} %entry_in.1, s32[32]{0:T(128)} %suffix_in.1, f32[16]{0:T(128)} %decay_in.1, f32[16]{0:T(128)} %bias_in.1, f32[16]{0:T(128)} %skip_in.1, ...), custom_call_target="tpu_custom_call" | custom-call | tf_op jit(solution)/shard_map/prefill/pallas_call | solution.py:705
  96.7 0.0 copy-start
  96.7 2.3 %copy.21 = bf16[1,64,8192]{2,1,0:T(8,128)(2,1)} copy(bf16[1,64,8192]{2,1,0:T(8,128)(2,1)} %bitcast.13) | data formatting | bytes 2097152
  99.0 0.0 copy-done
  99.0 0.8 copy.22
Async XLA Ops:
  96.7 2.3 %copy-start = (bf16[64,4096]{1,0:T(8,128)(2,1)S(1)}, bf16[64,4096]{1,0:T(8,128)(2,1)}, u32[]{:S(2)}) copy-start(bf16[64,4096]{1,0:T(8,128)(2,1)} %get-tuple-element.5) | copy-start | bytes 1572868

commit v3 on v2

--- a/solution.py
+++ b/solution.py
@@ -13,7 +13,7 @@
 ROWS = 64
 SPAN = 256
 PARTS = 8
-FLIGHT = 4
+FLIGHT = 6
 DIST = (0, 1, -1, 2, -2, 3, -3, 4)
 LOW = -1e30
 SCALE = 1.4426950408889634 / 128**0.5
@@ -57,7 +57,6 @@
     skip_gain,
     tabv,
     tabs,
-    bias,
     stepb,
     gainb,
     projb,
@@ -83,8 +82,10 @@
     tailb,
     osend,
     ob,
+    q2,
+    kk,
+    vt,
     m_s,
-    l_s,
     acc_s,
     ao,
     tsem,
@@ -312,15 +313,25 @@
         kv_hop(f, 1, -1)
     gather_state(0)
     gather_state(1)
-    in_step = everyone(0, step, stepb.at[my_rows, :])
-    in_proj = spread(1, proj, projb, 512)
-    in_x = spread(2, xin, xb, 1024)
-    for c in range(2, PARTS):
-        gather_state(c)
-    in_q = spread(3, query, qb, 512)
-    in_f = spread(4, fresh, fb, 256)
-    in_gain = everyone(5, gain, gainb.at[p])
-    in_gate = start_local(gate, gateb)
+    arrays = {}
+
+    def leave(name):
+        if name == "step":
+            arrays[name] = everyone(0, step, stepb.at[my_rows, :])
+        elif name == "proj":
+            arrays[name] = spread(1, proj, projb, 512)
+        elif name == "x":
+            arrays[name] = spread(2, xin, xb, 1024)
+        elif name == "q":
+            arrays[name] = spread(3, query, qb, 512)
+        elif name == "f":
+            arrays[name] = spread(4, fresh, fb, 256)
+        elif name == "gain":
+            arrays[name] = everyone(5, gain, gainb.at[p])
+        elif name == "gate":
+            arrays[name] = start_local(gate, gateb)
+
+    leave("step")
 
     for copy in small:
         copy.wait()
@@ -351,12 +362,6 @@
     live = suffix[r]
 
     side = lax.broadcasted_iota(jnp.int32, (1, 128), 1)
-    for k in range(8):
-        for t in range(NY):
-            word = tabs[lax.rem(z - DIST[k] + NZ, NZ) * NY + t, y]
-            flag = jnp.where(side < 64, lax.rem(lax.div(word, 16), 2), lax.div(word, 32))
-            place = (k % 2) * 512 + t * 128
-            bias[k // 2, :, place : place + 128] = jnp.where(flag > 0, 0.0, LOW)
 
     lower = lax.broadcasted_iota(jnp.int32, (SPAN, SPAN), 0) >= lax.broadcasted_iota(
         jnp.int32, (SPAN, SPAN), 1
@@ -364,7 +369,7 @@
     half = lax.broadcasted_iota(jnp.int32, (SPAN, 128), 1) < 64
 
     def scan_sums():
-        arrive(in_step)
+        arrive(arrays["step"])
         take = (
             lax.broadcasted_iota(jnp.int32, (128, 128), 0)
             == lax.broadcasted_iota(jnp.int32, (128, 128), 1) + p * 16
@@ -388,11 +393,11 @@
                 w_c[...] = jnp.exp(cum[SPAN - 1 : SPAN] - cum) * dt[rows]
 
     def scan_inner():
-        arrive(in_proj)
+        arrive(arrays["proj"])
         for b in range(2):
             rows = slice(b * SPAN, (b + 1) * SPAN)
             inner[b] = dot(projb[rows, 256:512], projb[rows, 0:256], BT)
-        arrive(in_x)
+        arrive(arrays["x"])
 
     def pair(hp, carry):
         cols = pl.ds(pl.multiple_of(hp * 128, 128), 128)
@@ -422,7 +427,7 @@
         add_s[...] = dot(projb[0:SPAN, 0:256], tailb[...], AT)
 
     def open_gate():
-        in_gate.wait()
+        arrays["gate"].wait()
 
         def some(g, carry):
             cols = pl.ds(pl.multiple_of(g * 1024, 1024), 1024)
@@ -468,68 +473,61 @@
             )
         ob[my_rows, cols] = osend[my_rows, cols]
 
-    def attend_fresh(i, carry):
-        head = i // 2
-        tile = lax.rem(i, 2)
-        qt = qb[pl.ds(pl.multiple_of(tile * 256, 256), 256), pl.ds(pl.multiple_of(head * 128, 128), 128)]
-        s = dot(qt, fb[:, 0:128], BT)
-        allowed = lax.broadcasted_iota(jnp.int32, (256, 512), 1) <= (
-            lax.broadcasted_iota(jnp.int32, (256, 512), 0) + tile * 256
+    def set_block(block, rows):
+        kk[0:rows, 0:128] = block[:, 0:128]
+        kk[0:rows, 128:256] = block[:, 0:128]
+        vt[0:128, 0:rows] = block[:, 128:256].T
+
+    def attend_first():
+        arrive(arrays["q"])
+        arrive(arrays["f"])
+        for head in range(4):
+            qf = qb[:, head * 128 : (head + 1) * 128].astype(F32) * SCALE
+            high = qf.astype(BF16)
+            q2[head, :, 0:128] = high
+            q2[head, :, 128:256] = (qf - high.astype(F32)).astype(BF16)
+        vt[128:144, :] = jnp.ones((16, 1024), BF16)
+        set_block(fb[...], 512)
+        allowed = lax.broadcasted_iota(jnp.int32, (512, 512), 0) <= lax.broadcasted_iota(
+            jnp.int32, (512, 512), 1
         )
-        s = jnp.where(allowed, s, LOW)
-        top = jnp.max(s, axis=1, keepdims=True)
-        w = jnp.exp2((s - top) * SCALE)
-        m_s[i] = jnp.broadcast_to(top, (256, 128))
-        l_s[i] = jnp.broadcast_to(jnp.sum(w, axis=1, keepdims=True), (256, 128))
-        acc_s[i] = dot(w.astype(BF16), fb[:, 128:256])
-        return carry
-
-    def attend_first():
-        arrive(in_q)
-        arrive(in_f)
-        lax.fori_loop(0, 8, attend_fresh, 0)
-
-    def attend_cached(n, lo, hi):
-        if lo == 0:
+        for head in range(4):
+            s = jnp.where(allowed, dot(kk[0:512, :], q2[head], BT), LOW)
+            top = jnp.max(s, axis=0, keepdims=True)
+            w = jnp.exp2(s - top).astype(BF16)
+            m_s[head] = jnp.broadcast_to(top, (8, 512))
+            acc_s[head] = dot(vt[:, 0:512], w)
+
+    def attend_cached(n, part):
+        if part == 0:
             for k in (2 * n, 2 * n + 1):
                 for j in range(1, NY):
                     kv_copies[k, j].wait_recv()
-
-        def tile_of(i, carry):
-            head = i // 2
-            tile = lax.rem(i, 2)
-            qt = qb[
-                pl.ds(pl.multiple_of(tile * 256, 256), 256), pl.ds(pl.multiple_of(head * 128, 128), 128)
-            ]
-            block = kvb[2 * n : 2 * n + 2].reshape(1024, 256)
-            s = dot(qt, block[:, 0:128], BT) + bias[n]
-            old = m_s[i][:, 0:1]
-            top = jnp.maximum(old, jnp.max(s, axis=1, keepdims=True))
-            w = jnp.exp2((s - top) * SCALE)
-            fade = jnp.exp2((old - top) * SCALE)
-            m_s[i] = jnp.broadcast_to(top, (256, 128))
-            l_s[i] = l_s[i] * fade + jnp.sum(w, axis=1, keepdims=True)
-            acc_s[i] = acc_s[i] * fade + dot(w.astype(BF16), block[:, 128:256])
-            return carry
-
-        lax.fori_loop(lo, hi, tile_of, 0)
+            set_block(kvb[2 * n : 2 * n + 2].reshape(1024, 256), 1024)
+        blocked = []
+        for k in (2 * n, 2 * n + 1):
+            for t in range(NY):
+                word = tabs[lax.rem(z - DIST[k] + NZ, NZ) * NY + t, y]
+                blocked.append(jnp.where(lax.rem(lax.div(word, 16), 2) > 0, 0.0, LOW))
+                blocked.append(jnp.where(lax.div(word, 32) > 0, 0.0, LOW))
+        for head in (2 * part, 2 * part + 1):
+            s = dot(kk[...], q2[head], BT)
+            s = jnp.concatenate([s[b * 64 : (b + 1) * 64] + blocked[b] for b in range(16)], axis=0)
+            old = m_s[head][0:1, :]
+            top = jnp.maximum(old, jnp.max(s, axis=0, keepdims=True))
+            w = jnp.exp2(s - top).astype(BF16)
+            m_s[head] = jnp.broadcast_to(top, (8, 512))
+            acc_s[head] = acc_s[head] * jnp.exp2(old - top) + dot(vt[...], w)
 
     my_cols = pl.ds(pl.multiple_of(p * 512, 512), 512)
     attn_sends = []
     own_attn = []
 
-    def finish(i, carry):
-        head = i // 2
-        tile = lax.rem(i, 2)
-        alive = lax.broadcasted_iota(jnp.int32, (256, 128), 0) + tile * 256 < live
-        value = jnp.where(alive, acc_s[i] / l_s[i], 0.0)
-        ao[
-            pl.ds(pl.multiple_of(tile * 256, 256), 256), pl.ds(pl.multiple_of(head * 128, 128), 128)
-        ] = value.astype(BF16)
-        return carry
-
     def attend_last():
-        lax.fori_loop(0, 8, finish, 0)
+        alive = lax.broadcasted_iota(jnp.int32, (128, 512), 1) < live
+        for head in range(4):
+            value = jnp.where(alive, acc_s[head, 0:128] / acc_s[head, 128:129], 0.0)
+            ao[:, head * 128 : (head + 1) * 128] = value.T.astype(BF16)
         for d in range(1, NT):
             to = tp_of(d)
             attn_sends.append(
@@ -569,12 +567,17 @@
             attend_cached(*args)
         elif name == "finish":
             attend_last()
+        elif name == "leave":
+            leave(*args)
+        elif name == "gather":
+            for c in range(*args):
+                gather_state(c)
         elif name == "add":
             scan_add()
         elif name == "gate":
             open_gate()
         elif name == "gain":
-            arrive(in_gain)
+            arrive(arrays["gain"])
         elif name == "drain":
             while pending[0] is not marks[args[0]]:
                 pending.pop(0).wait_send()
@@ -645,23 +648,34 @@
         copy.wait_send()
 
 
-BUDGET = 3.5
+BUDGET = 4.5
 COST = {
+    "leave": 0.5,
+    "gather": 0.4,
     "sums": 1.0,
     "inner": 0.5,
     "pair": 1.5,
     "add": 0.6,
     "carry": 1.2,
-    "fresh": 4.0,
-    "cached": 1.6,
+    "fresh": 2.5,
+    "cached": 2.0,
     "finish": 1.0,
     "gate": 1.2,
     "gain": 0.1,
     "drain": 0.3,
 }
 WORK = (
+    (1, "leave", "proj"),
+    (1, "leave", "x"),
+    (1, "gather", 2, 4),
+    (2, "gather", 4, 6),
+    (2, "leave", "q"),
+    (2, "leave", "f"),
+    (3, "gather", 6, 8),
+    (3, "leave", "gain"),
+    (3, "leave", "gate"),
     (3, "sums"),
-    (3, "gate"),
+    (4, "gate"),
     (4, "inner"),
     (4, "pair", 0, 2),
     (4, "pair", 2, 4),
@@ -673,24 +687,16 @@
     (6, "fresh"),
     (6, "carry", 2, 4),
     (7, "drain", 1),
-    (7, "cached", 0, 0, 2),
-    (7, "cached", 0, 2, 4),
-    (7, "cached", 0, 4, 6),
-    (7, "cached", 0, 6, 8),
+    (7, "cached", 0, 0),
+    (7, "cached", 0, 1),
     (8, "carry", 4, 6),
-    (8, "cached", 1, 0, 2),
-    (8, "cached", 1, 2, 4),
-    (8, "cached", 1, 4, 6),
-    (8, "cached", 1, 6, 8),
+    (8, "cached", 1, 0),
+    (8, "cached", 1, 1),
     (9, "drain", 4),
-    (9, "cached", 2, 0, 2),
-    (9, "cached", 2, 2, 4),
-    (9, "cached", 2, 4, 6),
-    (9, "cached", 2, 6, 8),
-    (10, "cached", 3, 0, 2),
-    (10, "cached", 3, 2, 4),
-    (10, "cached", 3, 4, 6),
-    (10, "cached", 3, 6, 8),
+    (9, "cached", 2, 0),
+    (9, "cached", 2, 1),
+    (10, "cached", 3, 0),
+    (10, "cached", 3, 1),
     (10, "finish"),
     (11, "drain", 8),
     (12, "carry", 6, 7),
@@ -721,7 +727,6 @@
             pltpu.SMEM((16,), F32),
             pltpu.VMEM((NZ * NY, 128), jnp.int32),
             pltpu.SMEM((NZ * NY, 128), jnp.int32),
-            pltpu.VMEM((4, 1, 1024), F32),
             pltpu.VMEM((512, 128), BF16),
             pltpu.VMEM((NT, 8, 128), F32),
             pltpu.VMEM((512, 512), BF16),
@@ -747,9 +752,11 @@
             pltpu.VMEM((256, 1024), BF16),
             pltpu.VMEM((512, 1024), BF16),
             pltpu.VMEM((512, 1024), BF16),
-            pltpu.VMEM((8, 256, 128), F32),
-            pltpu.VMEM((8, 256, 128), F32),
-            pltpu.VMEM((8, 256, 128), F32),
+            pltpu.VMEM((4, 512, 256), BF16),
+            pltpu.VMEM((1024, 256), BF16),
+            pltpu.VMEM((144, 1024), BF16),
+            pltpu.VMEM((4, 8, 512), F32),
+            pltpu.VMEM((4, 144, 512), F32),
             pltpu.VMEM((512, 512), BF16),
             dma((9,)),
             dma((24,)),

time: 99.9 us -> 89.3 us (0.89)
  Pallas kernels: 96.1 us -> 85.4 us
    pallas_call x1, Pallas kernels: 96.1 us -> 85.4 us  [run(): pl.pallas_call(kernel, out_shape=(jax.ShapeDtypeStruct((ROWS, 8192), BF16...]
where the time goes in v3:
time: 89.3 us; the launch traced here: 89.2 us
  Pallas kernels  85.4 us (96%)
  local copies, waits for them, and re-layouts  3.12 us (3%)
    pallas_call x1, Pallas kernels, run(): pl.pallas_call(kernel, out_shape=(jax.ShapeDtypeStruct((ROWS, 8192), BF16...  85.4 us
    unnamed x4, local copies, waits for them, and re-layouts  3.12 us

profile of v3, /device:TPU:1, one launch (start us, length us, event | category | flops | bytes accessed | tf_op | source)
XLA Modules:
  0.0 89.2 jit_solution(5434968332930933013)
XLA Ops:
  0.6 85.4 %prefill.1 = (bf16[64,8192]{1,0:T(8,128)(2,1)}, bf16[64,4096]{1,0:T(8,128)(2,1)}) custom-call(s32[32,64]{1,0:T(8,128)} %owner_in.1, s32[32,64]{1,0:T(8,128)} %slot_in.1, s32[32]{0:T(128)} %count_in.1, s32[32]{0:T(128)} %entry_in.1, s32[32]{0:T(128)} %suffix_in.1, f32[16]{0:T(128)} %decay_in.1, f32[16]{0:T(128)} %bias_in.1, f32[16]{0:T(128)} %skip_in.1, ...), custom_call_target="tpu_custom_call" | custom-call | tf_op jit(solution)/shard_map/prefill/pallas_call | solution.py:711
  86.1 0.0 copy-start
  86.1 2.3 %copy.21 = bf16[1,64,8192]{2,1,0:T(8,128)(2,1)} copy(bf16[1,64,8192]{2,1,0:T(8,128)(2,1)} %bitcast.13) | data formatting | bytes 2097152
  88.4 0.0 copy-done
  88.4 0.8 copy.22
Async XLA Ops:
  86.1 2.3 %copy-start = (bf16[64,4096]{1,0:T(8,128)(2,1)S(1)}, bf16[64,4096]{1,0:T(8,128)(2,1)}, u32[]{:S(2)}) copy-start(bf16[64,4096]{1,0:T(8,128)(2,1)} %get-tuple-element.5) | copy-start | bytes 1572868

commit v4 on v3

--- a/solution.py
+++ b/solution.py
@@ -615,6 +615,11 @@
     for item in list(work):
         do(item)
 
+    own_attn[0].wait()
+    for copy in attn_sends:
+        copy.wait_recv()
+    for copy in pending:
+        copy.wait_send()
     for copy in ssm_sends:
         copy.wait_recv()
 
@@ -640,12 +645,6 @@
         return carry
 
     lax.fori_loop(0, NT, norm, 0)
-
-    own_attn[0].wait()
-    for copy in attn_sends:
-        copy.wait_recv()
-    for copy in pending:
-        copy.wait_send()
 
 
 BUDGET = 4.5

time: 89.3 us -> 89.2 us (level)
  no operation moved by 1% of the time
where the time goes in v4:
time: 89.2 us; the launch traced here: 89.1 us
  Pallas kernels  85.3 us (96%)
  local copies, waits for them, and re-layouts  3.12 us (3%)
    pallas_call x1, Pallas kernels, run(): pl.pallas_call(kernel, out_shape=(jax.ShapeDtypeStruct((ROWS, 8192), BF16...  85.3 us
    unnamed x4, local copies, waits for them, and re-layouts  3.12 us

profile of v4, /device:TPU:1, one launch (start us, length us, event | category | flops | bytes accessed | tf_op | source)
XLA Modules:
  0.0 89.1 jit_solution(5022286785338005406)
XLA Ops:
  0.6 85.3 %prefill.1 = (bf16[64,8192]{1,0:T(8,128)(2,1)}, bf16[64,4096]{1,0:T(8,128)(2,1)}) custom-call(s32[32,64]{1,0:T(8,128)} %owner_in.1, s32[32,64]{1,0:T(8,128)} %slot_in.1, s32[32]{0:T(128)} %count_in.1, s32[32]{0:T(128)} %entry_in.1, s32[32]{0:T(128)} %suffix_in.1, f32[16]{0:T(128)} %decay_in.1, f32[16]{0:T(128)} %bias_in.1, f32[16]{0:T(128)} %skip_in.1, ...), custom_call_target="tpu_custom_call" | custom-call | tf_op jit(solution)/shard_map/prefill/pallas_call | solution.py:710
  86.0 0.0 copy-start
  86.0 2.3 %copy.21 = bf16[1,64,8192]{2,1,0:T(8,128)(2,1)} copy(bf16[1,64,8192]{2,1,0:T(8,128)(2,1)} %bitcast.13) | data formatting | bytes 2097152
  88.3 0.0 copy-done
  88.3 0.8 copy.22
Async XLA Ops:
  86.0 2.3 %copy-start = (bf16[64,4096]{1,0:T(8,128)(2,1)S(1)}, bf16[64,4096]{1,0:T(8,128)(2,1)}, u32[]{:S(2)}) copy-start(bf16[64,4096]{1,0:T(8,128)(2,1)} %get-tuple-element.5) | copy-start | bytes 1572868
